TPU v7x, 32 devices: a whole 2x2x4 slice. The times are simulated.
32 devices in a mesh: fsdp: 4 (over y, core), seq: 8 (over z, x).
Axes of the slice: x: 2, y: 2, z: 4, core: 2. Of those that a mesh axis runs over, the one named last changes fastest.
Arguments:
- hidden_in: bfloat16 [8, 1024, 2048], P('fsdp', 'seq'), may hold values from -6 to 6
- cotangent: bfloat16 [8, 1024, 2048], P('fsdp', 'seq'), may hold values from -6 to 6
- lengths: int32 [8], P('fsdp'), may hold values from 256 to 1024, as said below
- norm_gain: float32 [2048], replicated, may hold values from 0.5 to 1.5
- w_in: bfloat16 [2048, 8192], P('fsdp'), may hold values from -0.125 to 0.125
- conv_w: float32 [4, 4096], P(None, 'seq'), may hold values from -3 to 3
- conv_b: float32 [4096], P('seq'), may hold values from -1 to 1
- x_proj: bfloat16 [160, 4096], P(None, 'seq'), may hold values from -0.09375 to 0.09375
- dt_proj_w: bfloat16 [128, 4096], P(None, 'seq'), may hold values from -0.5 to 0.5
- dt_bias: float32 [4096], P('seq'), may hold values from -4.5 to -1
- a_log: float32 [16, 4096], P(None, 'seq'), may hold values from 0 to 2.77
- d_skip: float32 [4096], P('seq'), may hold values from 0.5 to 1.5
- w_out: bfloat16 [2048, 4096], P('fsdp'), may hold values from -0.1875 to 0.1875
Outputs:
- block_out: bfloat16 [8, 1024, 2048], P('fsdp', 'seq')
- grad_in: bfloat16 [8, 1024, 2048], P('fsdp', 'seq')
- grad_gain: float32 [2048], replicated
- grad_w_in: float32 [2048, 8192], P(('fsdp', 'seq'))
- grad_conv_w: float32 [4, 4096], P(None, 'seq')
- grad_conv_b: float32 [4096], P('seq')
- grad_x_proj: float32 [160, 4096], P(None, 'seq')
- grad_dt_proj: float32 [128, 4096], P(None, 'seq')
- grad_dt_bias: float32 [4096], P('seq')
- grad_a_log: float32 [16, 4096], P(None, 'seq')
- grad_d_skip: float32 [4096], P('seq')
- grad_w_out: float32 [2048, 4096], P(('fsdp', 'seq'))
Inputs may be any that keep to these rules, and one draw needn't show every extreme that they name: `lengths`: sequence g * 2 + m is micro-batch m of index g of fsdp; in every index one of its 2 sequences has all 1024 positions, and some sequence has exactly 256.
All inputs are finite; a program needn't handle non-finite values.
Results may differ from a plain program's by a relative error of at most 0.012.
Values may be sent and summed in bfloat16 or wider, within the bound.
No kernel may reach another device: no remote copies, remote signals or barrier semaphores. Data moves between devices by JAX's collectives and lax.ppermute only.
A program may use at most 304 MiB of HBM per device.

v0:
```python
from functools import partial

import jax
import jax.numpy as jnp
from jax import lax
from jax.sharding import PartitionSpec as P

EPS = 1e-05
DOT_ROWS = (((0,), (0,)), ((), ()))
DOT_COLS = (((1,), (1,)), ((), ()))
DOT_PLAIN = (((1,), (0,)), ((), ()))


def silu_slope(values):
    sigmoid_value = jax.nn.sigmoid(values)
    return sigmoid_value * (1.0 + values * (1.0 - sigmoid_value))


def split_blocks(values, block_count):
    return values.reshape((block_count, values.shape[0] // block_count) + values.shape[1:])


def split_columns(values, block_count):
    return jnp.swapaxes(
        values.reshape(values.shape[0], block_count, values.shape[1] // block_count), 0, 1
    )


def forward_stretch(rates, carried, pieces):
    step_sizes, step_input, step_entry, step_readout = pieces

    def one_row(hidden, row_values):
        row_size, row_input, row_entry, row_readout = row_values
        hidden = (
            jnp.exp(row_size[None, :] * rates) * hidden
            + row_entry[:, None] * (row_size * row_input)[None, :]
        )
        return (hidden, jnp.sum(row_readout[:, None] * hidden, axis=0))

    final_state, outputs = lax.scan(
        one_row, carried, (step_sizes, step_input, step_entry.T, step_readout.T), unroll=16
    )
    return (final_state, (outputs, carried))


def backward_stretch(rates, carried, pieces):
    step_sizes, step_input, step_entry, step_readout, step_grad, start_state = pieces
    entry_cols = step_entry.T
    readout_cols = step_readout.T

    def replay_row(hidden, row_values):
        row_size, row_input, row_entry, row_grad = row_values
        earlier = hidden
        hidden = (
            jnp.exp(row_size[None, :] * rates) * hidden
            + row_entry[:, None] * (row_size * row_input)[None, :]
        )
        return (hidden, (earlier, jnp.sum(hidden * row_grad[None, :], axis=1)))

    _, (earlier_states, readout_grad) = lax.scan(
        replay_row, start_state, (step_sizes, step_input, entry_cols, step_grad), unroll=16
    )

    def back_row(carry_values, row_values):
        later_grad, decay_total = carry_values
        row_size, row_input, row_entry, row_readout, row_grad, earlier = row_values
        decay_rate = jnp.exp(row_size[None, :] * rates)
        state_grad = row_readout[:, None] * row_grad[None, :] + later_grad
        log_grad = state_grad * earlier * decay_rate
        shared = jnp.sum(state_grad * row_entry[:, None], axis=0)
        size_grad = jnp.sum(log_grad * rates, axis=0) + shared * row_input
        input_grad = shared * row_size
        entry_grad = jnp.sum(state_grad * (row_size * row_input)[None, :], axis=1)
        decay_total = decay_total + log_grad * row_size[None, :]
        return ((decay_rate * state_grad, decay_total), (size_grad, input_grad, entry_grad))

    start_carry = (carried, jnp.zeros_like(carried))
    (passed_grad, decay_grad), (size_grad, input_grad, entry_grad) = lax.scan(
        back_row,
        start_carry,
        (step_sizes, step_input, entry_cols, readout_cols, step_grad, earlier_states),
        reverse=True,
        unroll=16,
    )
    return (passed_grad, (size_grad, input_grad, decay_grad, entry_grad, readout_grad))


def channel_forward(x_sent, params):
    conv_w, conv_b, x_proj, dt_proj_w, dt_bias, rates, d_skip = params
    seq_length, chan_width = x_sent.shape
    conv_taps = conv_w.shape[0]
    low_rank = dt_proj_w.shape[0]
    state_count = rates.shape[0]
    padded = jnp.concatenate(
        [jnp.zeros((conv_taps - 1, chan_width), jnp.float32), x_sent.astype(jnp.float32)], axis=0
    )
    pre_conv = conv_b + sum(
        (conv_w[offset] * padded[offset : offset + seq_length] for offset in range(conv_taps))
    )
    u_act = jax.nn.silu(pre_conv).astype(jnp.bfloat16)
    select_part = lax.dot_general(x_proj, u_act, DOT_COLS, preferred_element_type=jnp.float32)
    select = lax.psum(select_part, "seq")
    size_low = select[:low_rank].astype(jnp.bfloat16)
    entry_rows = select[low_rank : low_rank + state_count]
    readout_rows = select[low_rank + state_count :]
    size_pre = (
        lax.dot_general(size_low, dt_proj_w, DOT_ROWS, preferred_element_type=jnp.float32) + dt_bias
    )
    step_sizes = jax.nn.softplus(size_pre)
    u_float = u_act.astype(jnp.float32)
    block_count = seq_length // min(256, seq_length)
    pieces = (
        split_blocks(step_sizes, block_count),
        split_blocks(u_float, block_count),
        split_columns(entry_rows, block_count),
        split_columns(readout_rows, block_count),
    )
    initial = jnp.zeros((state_count, chan_width), jnp.float32)
    _, (scanned, starts) = lax.scan(partial(forward_stretch, rates), initial, pieces)
    scanned = scanned.reshape(seq_length, chan_width) + d_skip * u_float
    saved_state = (padded, pre_conv, u_act, size_low, size_pre, pieces, starts)
    return (scanned.astype(jnp.bfloat16), saved_state)


def channel_backward(grad_sent, saved_state, params):
    conv_w, conv_b, x_proj, dt_proj_w, dt_bias, rates, d_skip = params
    padded, pre_conv, u_act, size_low, size_pre, pieces, starts = saved_state
    seq_length, chan_width = pre_conv.shape
    conv_taps = conv_w.shape[0]
    block_count = pieces[0].shape[0]
    grad_float = grad_sent.astype(jnp.float32)
    initial = jnp.zeros((rates.shape[0], chan_width), jnp.float32)
    scan_inputs = pieces + (split_blocks(grad_float, block_count), starts)
    _, (size_grad, input_grad, decay_grad, entry_grad, readout_grad) = lax.scan(
        partial(backward_stretch, rates), initial, scan_inputs, reverse=True
    )
    size_grad = size_grad.reshape(seq_length, chan_width)
    pre_grad = (size_grad * jax.nn.sigmoid(size_pre)).astype(jnp.bfloat16)
    bias_grad = jnp.sum(pre_grad.astype(jnp.float32), axis=0)
    proj_grad = lax.dot_general(size_low, pre_grad, DOT_PLAIN, preferred_element_type=jnp.float32)
    low_grad = lax.dot_general(dt_proj_w, pre_grad, DOT_COLS, preferred_element_type=jnp.float32)
    entry_flat = entry_grad.reshape(seq_length, entry_grad.shape[2]).T
    readout_flat = readout_grad.reshape(seq_length, readout_grad.shape[2]).T
    select_part = jnp.concatenate([low_grad, entry_flat, readout_flat], axis=0)
    select_grad = lax.psum(select_part, "seq").astype(jnp.bfloat16)
    xproj_grad = lax.dot_general(select_grad, u_act, DOT_PLAIN, preferred_element_type=jnp.float32)
    u_float = u_act.astype(jnp.float32)
    u_grad = (
        input_grad.reshape(seq_length, chan_width)
        + d_skip * grad_float
        + lax.dot_general(select_grad, x_proj, DOT_ROWS, preferred_element_type=jnp.float32)
    )
    skip_grad = jnp.sum(grad_float * u_float, axis=0)
    conv_grad = u_grad * silu_slope(pre_conv)
    convb_grad = jnp.sum(conv_grad, axis=0)
    convw_grad = jnp.stack(
        [
            jnp.sum(conv_grad * padded[offset : offset + seq_length], axis=0)
            for offset in range(conv_taps)
        ]
    )
    grad_padded = jnp.concatenate(
        [conv_grad, jnp.zeros((conv_taps - 1, chan_width), jnp.float32)], axis=0
    )
    x_grad = sum(
        (
            conv_w[offset]
            * grad_padded[conv_taps - 1 - offset : conv_taps - 1 - offset + seq_length]
            for offset in range(conv_taps)
        )
    )
    decay_total = jnp.sum(decay_grad, axis=0) * rates
    return (
        x_grad.astype(jnp.bfloat16),
        (convw_grad, convb_grad, xproj_grad, proj_grad, bias_grad, decay_total, skip_grad),
    )


def token_group(hidden_group, cot_group, valid_group, norm_gain, w_in, w_out, params):
    group_size, rows_dev, model_width = hidden_group.shape
    in_full, out_full = (
        lax.all_gather(w_in, "fsdp", axis=0, tiled=True),
        lax.all_gather(w_out, "fsdp", axis=0, tiled=True),
    )
    flat_rows = hidden_group.reshape(group_size * rows_dev, model_width).astype(jnp.float32)
    inverse = lax.rsqrt(jnp.mean(flat_rows * flat_rows, axis=-1, keepdims=True) + EPS)
    scaled = flat_rows * inverse
    normed = (scaled * norm_gain).astype(jnp.bfloat16)
    projected = jnp.dot(normed, in_full, preferred_element_type=jnp.float32)
    inner_width = in_full.shape[1] // 2
    x_tokens = projected[:, :inner_width].astype(jnp.bfloat16)
    z_part = projected[:, inner_width:]
    x_sent = lax.all_to_all(x_tokens, "seq", split_axis=1, concat_axis=0, tiled=True)
    y_sent, saved_state = channel_forward(x_sent, params)
    y_pieces = lax.all_to_all(y_sent, "seq", split_axis=0, concat_axis=1, tiled=True)
    y_tokens = y_pieces.astype(jnp.float32)
    z_gate = jax.nn.silu(z_part)
    gated = (y_tokens * z_gate).astype(jnp.bfloat16)
    branch = lax.dot_general(gated, out_full, DOT_COLS, preferred_element_type=jnp.float32)
    valid_flat = valid_group.reshape(-1, 1)
    block_out = (flat_rows + valid_flat * branch).astype(jnp.bfloat16)
    cot_flat = cot_group.reshape(group_size * rows_dev, model_width).astype(jnp.float32)
    branch_grad = (cot_flat * valid_flat).astype(jnp.bfloat16)
    gated_grad = jnp.dot(branch_grad, out_full, preferred_element_type=jnp.float32)
    y_grad = (gated_grad * z_gate).astype(jnp.bfloat16)
    z_low = (gated_grad * y_tokens * silu_slope(z_part)).astype(jnp.bfloat16)
    grad_sent = lax.all_to_all(y_grad, "seq", split_axis=1, concat_axis=0, tiled=True)
    x_grad, channel_grads = channel_backward(grad_sent, saved_state, params)
    x_pieces = lax.all_to_all(x_grad, "seq", split_axis=0, concat_axis=1, tiled=True)
    both_grad = jnp.concatenate([x_pieces, z_low], axis=1)
    normed_grad = lax.dot_general(both_grad, in_full, DOT_COLS, preferred_element_type=jnp.float32)
    gain_part = jnp.sum(normed_grad * scaled, axis=0)
    scaled_grad = normed_grad * norm_gain
    grad_rows = cot_flat + inverse * (
        scaled_grad - scaled * jnp.mean(scaled_grad * scaled, axis=-1, keepdims=True)
    )
    weight_terms = (normed, both_grad, gated, branch_grad)
    return (
        block_out.reshape(hidden_group.shape),
        grad_rows.astype(jnp.bfloat16).reshape(hidden_group.shape),
        weight_terms,
        channel_grads,
        gain_part,
    )


def shards(
    hidden_in,
    cotangent,
    lengths,
    norm_gain,
    w_in,
    conv_w,
    conv_b,
    x_proj,
    dt_proj_w,
    dt_bias,
    a_log,
    d_skip,
    w_out,
):
    micro_count, rows_dev, model_width = hidden_in.shape
    params = (conv_w, conv_b, x_proj, dt_proj_w, dt_bias, -jnp.exp(a_log), d_skip)
    positions = lax.axis_index("seq") * rows_dev + jnp.arange(rows_dev, dtype=jnp.int32)
    valid_rows = (positions[None, :] < lengths[:, None]).astype(jnp.float32)
    bounds = [(micro_index, micro_index + 1) for micro_index in range(micro_count)]
    outcomes = [
        token_group(
            hidden_in[low_index:high_index],
            cotangent[low_index:high_index],
            valid_rows[low_index:high_index],
            norm_gain,
            w_in,
            w_out,
            params,
        )
        for low_index, high_index in bounds
    ]
    block_out = jnp.concatenate([outcome[0] for outcome in outcomes], axis=0)
    grad_in = jnp.concatenate([outcome[1] for outcome in outcomes], axis=0)
    channel_total = outcomes[0][3]
    gain_total = outcomes[0][4]
    for outcome in outcomes[1:]:
        channel_total = tuple(
            (running_sum + latest_sum for running_sum, latest_sum in zip(channel_total, outcome[3]))
        )
        gain_total = gain_total + outcome[4]
    normed_all = jnp.concatenate([outcome[2][0] for outcome in outcomes], axis=0)
    both_all = jnp.concatenate([outcome[2][1] for outcome in outcomes], axis=0)
    gated_all = jnp.concatenate([outcome[2][2] for outcome in outcomes], axis=0)
    branch_all = jnp.concatenate([outcome[2][3] for outcome in outcomes], axis=0)
    inner_part = lax.dot_general(normed_all, both_all, DOT_ROWS, preferred_element_type=jnp.float32)
    outer_part = lax.dot_general(
        branch_all, gated_all, DOT_ROWS, preferred_element_type=jnp.float32
    )
    joint_rows = lax.psum_scatter(
        jnp.concatenate([inner_part, outer_part], axis=1),
        ("fsdp", "seq"),
        scatter_dimension=0,
        tiled=True,
    )
    grad_w_in = joint_rows[:, : w_in.shape[1]]
    grad_w_out = joint_rows[:, w_in.shape[1] :]
    convw_part, convb_part, xproj_part, proj_part, bias_part, decay_part, skip_part = channel_total
    convw_sum, convb_sum, xproj_sum, proj_sum, bias_sum, decay_sum, skip_sum = lax.psum(
        (convw_part, convb_part, xproj_part, proj_part, bias_part, decay_part, skip_part), "fsdp"
    )
    grad_gain = lax.psum(gain_total, ("fsdp", "seq"))
    return (
        block_out,
        grad_in,
        grad_gain,
        grad_w_in,
        convw_sum,
        convb_sum,
        xproj_sum,
        proj_sum,
        bias_sum,
        decay_sum,
        skip_sum,
        grad_w_out,
    )


def solution(mesh):
    return jax.shard_map(
        shards,
        mesh=mesh,
        in_specs=(
            P("fsdp", "seq", None),
            P("fsdp", "seq", None),
            P("fsdp"),
            P(),
            P("fsdp", None),
            P(None, "seq"),
            P("seq"),
            P(None, "seq"),
            P(None, "seq"),
            P("seq"),
            P(None, "seq"),
            P("seq"),
            P("fsdp", None),
        ),
        out_specs=(
            P("fsdp", "seq", None),
            P("fsdp", "seq", None),
            P(),
            P(("fsdp", "seq"), None),
            P(None, "seq"),
            P("seq"),
            P(None, "seq"),
            P(None, "seq"),
            P("seq"),
            P(None, "seq"),
            P("seq"),
            P(("fsdp", "seq"), None),
        ),
        check_vma=False,
    )
```

profile of v0, /device:TPU:0, one launch (start us, length us, event | category | flops | bytes accessed | tf_op | source)
XLA Modules:
  0.0 5468.2 jit_solution(3606325303470678573)
XLA Ops:
  10.4 203.4 %all-gather.3.cloned.1.call-done = bf16[2048,8192]{1,0:T(8,128)(2,1)} async-done(((bf16[512,8192]{1,0:T(8,128)(2,1)}), bf16[2048,8192]{1,0:T(8,128)(2,1)}) %all-gather.3.cloned.1.call-update) | async-done | bytes 33554448 | tf_op jit(solution)/shard_map/all_gather | solution.py:182
  213.9 14.6 fusion.381
  238.5 82.9 %all-gather.5.cloned.1.call-done = bf16[2048,4096]{1,0:T(8,128)(2,1)} async-done(((bf16[512,4096]{1,0:T(8,128)(2,1)}), bf16[2048,4096]{1,0:T(8,128)(2,1)}) %all-gather.5.cloned.1.call-update) | async-done | bytes 16777232 | tf_op jit(solution)/shard_map/all_gather | solution.py:183
  338.3 12.9 fusion.382
  379.9 14.3 all-to-all-done.2
  401.9 22.3 all-to-all-done.6
  444.8 74.1 %all-reduce.12.cloned.1.call-done = (f32[160,1024]{1,0:T(8,128)}, f32[160,1024]{1,0:T(8,128)}) async-done(((f32[160,1024]{1,0:T(8,128)}, f32[160,1024]{1,0:T(8,128)}), (f32[160,1024]{1,0:T(8,128)}, f32[160,1024]{1,0:T(8,128)})) %all-reduce.12.cloned.1.call-update) | async-done | bytes 1310736 | tf_op jit(solution)/shard_map/psum | solution.py:102
  533.6 402.6 %while.293 = (s32[]{:T(128)}, f32[16,512]{1,0:T(8,128)S(1)}, f32[4,256,512]{2,1,0:T(8,128)}, f32[4,16,512]{2,1,0:T(8,128)}, f32[4,256,512]{2,1,0:T(8,128)S(1)}, ...) while((s32[]{:T(128)}, f32[16,512]{1,0:T(8,128)S(1)}, ...), condition=%wide.region_43.44_spmd, body=%wide.region_24.43_spmd.sunk | while | flops 1179667 | bytes 4251386 | solution.py:119
  537.0 95.4 %while.301 = (s32[]{:T(128)}, f32[16,512]{1,0:T(8,128)S(1)}, f32[16,16,512]{2,1,0:T(8,128)}, f32[16,16,512]{2,1,0:T(8,128)S(1)}, f32[16,512]{1,0:T(8,128)S(1)}, ...) while((s32[]{:T(128)}, f32[16,512]{1,0:T(8,128)S(1)}, ...), condition=%wide.region_42.42_spmd, body=%wide.region_25.41_spmd.sunk | while | flops 1179665 | bytes 974109 | solution.py:40
  637.6 95.4 %while.301 = (s32[]{:T(128)}, f32[16,512]{1,0:T(8,128)S(1)}, f32[16,16,512]{2,1,0:T(8,128)}, f32[16,16,512]{2,1,0:T(8,128)S(1)}, f32[16,512]{1,0:T(8,128)S(1)}, ...) while((s32[]{:T(128)}, f32[16,512]{1,0:T(8,128)S(1)}, ...), condition=%wide.region_42.42_spmd, body=%wide.region_25.41_spmd.sunk | while | flops 1179665 | bytes 974109 | solution.py:40
  738.3 95.4 %while.301 = (s32[]{:T(128)}, f32[16,512]{1,0:T(8,128)S(1)}, f32[16,16,512]{2,1,0:T(8,128)}, f32[16,16,512]{2,1,0:T(8,128)S(1)}, f32[16,512]{1,0:T(8,128)S(1)}, ...) while((s32[]{:T(128)}, f32[16,512]{1,0:T(8,128)S(1)}, ...), condition=%wide.region_42.42_spmd, body=%wide.region_25.41_spmd.sunk | while | flops 1179665 | bytes 974109 | solution.py:40
  838.9 95.4 %while.301 = (s32[]{:T(128)}, f32[16,512]{1,0:T(8,128)S(1)}, f32[16,16,512]{2,1,0:T(8,128)}, f32[16,16,512]{2,1,0:T(8,128)S(1)}, f32[16,512]{1,0:T(8,128)S(1)}, ...) while((s32[]{:T(128)}, f32[16,512]{1,0:T(8,128)S(1)}, ...), condition=%wide.region_42.42_spmd, body=%wide.region_25.41_spmd.sunk | while | flops 1179665 | bytes 974109 | solution.py:40
  938.6 168.6 %while.291 = (s32[]{:T(128)}, f32[16,512]{1,0:T(8,128)S(1)}, f32[4,256,512]{2,1,0:T(8,128)}, f32[4,16,512]{2,1,0:T(8,128)}, f32[4,256,512]{2,1,0:T(8,128)}, /*in...) while((s32[]{:T(128)}, f32[16,512]{1,0:T(8,128)S(1)}, ...), condition=%wide.region_21.22_spmd, body=%wide.region_2.21_spmd.sunk | while | flops 1179667 | bytes 4251386 | solution.py:119
  942.1 37.8 while.300
  984.2 37.8 while.300
  1026.4 37.8 while.300
  1068.5 37.8 while.300
  1112.7 1587.8 %while.296 = (s32[]{:T(128)}, f32[16,512]{1,0:T(8,128)S(1)}, f32[4,256,512]{2,1,0:T(8,128)}, f32[4,256,512]{2,1,0:T(8,128)}, f32[4,16,512]{2,1,0:T(8,128)}, /*in...) while((s32[]{:T(128)}, f32[16,512]{1,0:T(8,128)S(1)}, ...), condition=%wide.region_113.114_spmd, body=%wide.region_44.113_spmd.sunk | while | flops 4226599 | bytes 14257481 | solution.py:134
  1119.0 50.4 while.302
  1169.5 338.1 %while.303 = (s32[]{:T(128)}, f32[16,512]{1,0:T(8,128)S(1)}, f32[16,512]{1,0:T(8,128)S(1)}, f32[16,16,512]{2,1,0:T(8,128)S(1)}, f32[16,16,512]{2,1,0:T(8,128)S(1...) while((s32[]{:T(128)}, f32[16,512]{1,0:T(8,128)S(1)}, ...), condition=%wide.region_112.112_spmd.clone, body=%wide.region_63.111_spmd.clone.sunk | while | flops 2907923 | bytes 3841291 | solution.py:78
  1515.9 50.4 while.302
  1566.4 338.1 %while.303 = (s32[]{:T(128)}, f32[16,512]{1,0:T(8,128)S(1)}, f32[16,512]{1,0:T(8,128)S(1)}, f32[16,16,512]{2,1,0:T(8,128)S(1)}, f32[16,16,512]{2,1,0:T(8,128)S(1...) while((s32[]{:T(128)}, f32[16,512]{1,0:T(8,128)S(1)}, ...), condition=%wide.region_112.112_spmd.clone, body=%wide.region_63.111_spmd.clone.sunk | while | flops 2907923 | bytes 3841291 | solution.py:78
  1912.7 50.4 while.302
  1963.2 338.1 %while.303 = (s32[]{:T(128)}, f32[16,512]{1,0:T(8,128)S(1)}, f32[16,512]{1,0:T(8,128)S(1)}, f32[16,16,512]{2,1,0:T(8,128)S(1)}, f32[16,16,512]{2,1,0:T(8,128)S(1...) while((s32[]{:T(128)}, f32[16,512]{1,0:T(8,128)S(1)}, ...), condition=%wide.region_112.112_spmd.clone, body=%wide.region_63.111_spmd.clone.sunk | while | flops 2907923 | bytes 3841291 | solution.py:78
  2309.6 50.4 while.302
  2360.1 338.1 %while.303 = (s32[]{:T(128)}, f32[16,512]{1,0:T(8,128)S(1)}, f32[16,512]{1,0:T(8,128)S(1)}, f32[16,16,512]{2,1,0:T(8,128)S(1)}, f32[16,16,512]{2,1,0:T(8,128)S(1...) while((s32[]{:T(128)}, f32[16,512]{1,0:T(8,128)S(1)}, ...), condition=%wide.region_112.112_spmd.clone, body=%wide.region_63.111_spmd.clone.sunk | while | flops 2907923 | bytes 3841291 | solution.py:78
  2709.8 1588.0 %while.299 = (s32[]{:T(128)}, f32[16,512]{1,0:T(8,128)S(1)}, f32[4,256,512]{2,1,0:T(8,128)}, f32[4,256,512]{2,1,0:T(8,128)}, f32[4,16,512]{2,1,0:T(8,128)}, /*in...) while((s32[]{:T(128)}, f32[16,512]{1,0:T(8,128)S(1)}, ...), condition=%wide.region_185.186_spmd, body=%wide.region_116.185_spmd.sunk | while | flops 4226599 | bytes 14257481 | solution.py:134
  2715.7 50.4 while.304
  2766.2 338.2 %while.305 = (s32[]{:T(128)}, f32[16,512]{1,0:T(8,128)S(1)}, f32[16,512]{1,0:T(8,128)S(1)}, f32[16,16,512]{2,1,0:T(8,128)S(1)}, f32[16,16,512]{2,1,0:T(8,128)S(1...) while((s32[]{:T(128)}, f32[16,512]{1,0:T(8,128)S(1)}, ...), condition=%wide.region_184.184_spmd.clone, body=%wide.region_135.183_spmd.clone.sunk | while | flops 2907923 | bytes 3841291 | solution.py:78
  3112.7 50.4 while.304
  3163.2 338.2 %while.305 = (s32[]{:T(128)}, f32[16,512]{1,0:T(8,128)S(1)}, f32[16,512]{1,0:T(8,128)S(1)}, f32[16,16,512]{2,1,0:T(8,128)S(1)}, f32[16,16,512]{2,1,0:T(8,128)S(1...) while((s32[]{:T(128)}, f32[16,512]{1,0:T(8,128)S(1)}, ...), condition=%wide.region_184.184_spmd.clone, body=%wide.region_135.183_spmd.clone.sunk | while | flops 2907923 | bytes 3841291 | solution.py:78
  3509.7 50.4 while.304
  3560.2 338.2 %while.305 = (s32[]{:T(128)}, f32[16,512]{1,0:T(8,128)S(1)}, f32[16,512]{1,0:T(8,128)S(1)}, f32[16,16,512]{2,1,0:T(8,128)S(1)}, f32[16,16,512]{2,1,0:T(8,128)S(1...) while((s32[]{:T(128)}, f32[16,512]{1,0:T(8,128)S(1)}, ...), condition=%wide.region_184.184_spmd.clone, body=%wide.region_135.183_spmd.clone.sunk | while | flops 2907923 | bytes 3841291 | solution.py:78
  3906.7 50.4 while.304
  3957.2 338.2 %while.305 = (s32[]{:T(128)}, f32[16,512]{1,0:T(8,128)S(1)}, f32[16,512]{1,0:T(8,128)S(1)}, f32[16,16,512]{2,1,0:T(8,128)S(1)}, f32[16,16,512]{2,1,0:T(8,128)S(1...) while((s32[]{:T(128)}, f32[16,512]{1,0:T(8,128)S(1)}, ...), condition=%wide.region_184.184_spmd.clone, body=%wide.region_135.183_spmd.clone.sunk | while | flops 2907923 | bytes 3841291 | solution.py:78
  4315.6 87.8 %all-reduce.15 = (bf16[160,1024]{1,0:T(8,128)(2,1)}, bf16[160,1024]{1,0:T(8,128)(2,1)S(1)}) all-reduce(f32[160,1024]{1,0:T(8,128)S(1)} %pad_maximum_fusion.4, f32[160,1024]{1,0:T(8,128)} %pad_maximum_fusion.3), channel_id=1, replica_groups=mesh['fsdp'=4,'seq'=8] {'seq'}, use_global_device_ids=true, to_apply=%region_186.187 | all-reduce | flops 327680 | bytes 1966080 | tf_op jit(solution)/shard_map/psum | solution.py:145
  4420.5 17.6 all-to-all-done.5
  4438.1 29.2 all_to_all.116
  4496.4 13.3 fusion.310
  4509.8 26.4 fusion.288
  4536.2 65.0 %pad_maximum_fusion = f32[2048,12288]{1,0:T(8,128)} fusion(f32[2048,4096]{1,0:T(8,128)} %fusion.310, f32[2048,8192]{1,0:T(8,128)} %fusion.288), kind=kLoop, calls=%fused_computation.1168 | loop fusion | flops 25165824 | bytes 201326592 | tf_op jit(solution)/shard_map/concatenate | solution.py:277
  4621.3 23.1 fusion.306
  4644.5 24.6 fusion.346
  4672.8 15.8 fusion.300
  4688.6 14.8 fusion.301
  4704.5 37.7 psum.88
  4743.2 679.0 %reduce-scatter.2.cloned.1.call-done = f32[64,12288]{1,0:T(8,128)} async-done(((f32[2048,12288]{1,0:T(8,128)}), f32[64,12288]{1,0:T(8,128)}) %reduce-scatter.2.cloned.1.call-update) | async-done | bytes 3145744 | tf_op jit(solution)/shard_map/reduce_scatter | solution.py:276
  5427.5 30.3 all-reduce.14.cloned.1.call-done
  (16713 shorter events, 3889.5 us)
Async XLA Ops:
  7.2 427.0 %copy-start = (bf16[160,512]{1,0:T(8,128)(2,1)S(1)}, bf16[160,512]{1,0:T(8,128)(2,1)}, u32[]{:S(2)}) copy-start(bf16[160,512]{1,0:T(8,128)(2,1)} %param.40) | copy-start | bytes 491524
  7.2 206.7 %all-gather.3.cloned.1.call-start = ((), (), s32[]{:S(2)}) async-start(), calls=%async_computation.9 | async-start | bytes 41943040 | tf_op jit(solution)/shard_map/all_gather | solution.py:182
  8.0 313.4 %all-gather.5.cloned.1.call-start = ((), (), s32[]{:S(2)}) async-start(), calls=%async_computation.10 | async-start | bytes 20971520 | tf_op jit(solution)/shard_map/all_gather | solution.py:183
  10.4 218.1 %copy-start.33 = (bf16[128,2048]{1,0:T(8,128)(2,1)}, bf16[128,2048]{1,0:T(8,128)(2,1)S(1)}, u32[]{:S(2)}) copy-start(bf16[128,2048]{1,0:T(8,128)(2,1)S(1)} %get-tuple-element.2637) | copy-start | bytes 1572868
  10.4 327.9 %copy-start.34 = (bf16[128,2048]{1,0:T(8,128)(2,1)}, bf16[128,2048]{1,0:T(8,128)(2,1)S(1)}, u32[]{:S(2)}) copy-start(bf16[128,2048]{1,0:T(8,128)(2,1)S(1)} %get-tuple-element.2638) | copy-start | bytes 1572868
  228.7 8.9 copy-start.38
  231.6 101.1 %all-to-all-start = ((bf16[128,8,512]{2,0,1:T(8,128)(2,1)}), bf16[128,8,512]{2,0,1:T(8,128)(2,1)S(1)}, u32[]{:S(2)}, u32[]{:S(2)}) async-start(bf16[128,8,512]{2,0,1:T(8,128)(2,1)} %bitcast.3456), calls=%async_computation | async-start | bytes 2097152 | tf_op jit(solution)/shard_map/all_to_all | solution.py:193
  238.5 93.3 %copy-start.41 = (bf16[128,2048]{1,0:T(8,128)(2,1)}, bf16[128,2048]{1,0:T(8,128)(2,1)S(1)}, u32[]{:S(2)}) copy-start(bf16[128,2048]{1,0:T(8,128)(2,1)S(1)} %get-tuple-element.2639) | copy-start | bytes 1572868
  332.8 65.8 %copy-start.16 = (bf16[128,8,512]{2,0,1:T(8,128)(2,1)}, bf16[128,8,512]{2,0,1:T(8,128)(2,1)S(1)}, u32[]{:S(2)}) copy-start(bf16[128,8,512]{2,0,1:T(8,128)(2,1)S(1)} %all-to-all-done) | copy-start | bytes 3145732
  332.8 31.7 all-to-all-start.4
  364.5 75.8 %copy-start.20 = (bf16[128,8,512]{2,0,1:T(8,128)(2,1)}, bf16[128,8,512]{2,0,1:T(8,128)(2,1)S(1)}, u32[]{:S(2)}) copy-start(bf16[128,8,512]{2,0,1:T(8,128)(2,1)S(1)} %all-to-all-done.4) | copy-start | bytes 3145732
  364.5 29.8 all-to-all-start.2
  378.9 19.7 copy-start.74
  394.3 6.0 copy-start.18
  394.3 29.9 all-to-all-start.6
  398.5 120.4 %all-reduce.12.cloned.1.call-start = ((), (), s32[]{:S(2)}) async-start(), calls=%async_computation.12 | async-start | bytes 2621440 | tf_op jit(solution)/shard_map/psum | solution.py:102
  398.6 25.6 copy-start.60
  398.6 25.5 copy-start.62
  398.6 25.5 copy-start.64
  398.7 25.5 copy-start.66
  400.3 23.9 copy-start.86
  434.2 4.5 copy-start.3
  444.8 80.0 %copy-start.48 = (bf16[128,512]{1,0:T(8,128)(2,1)S(1)}, bf16[128,512]{1,0:T(8,128)(2,1)}, u32[]{:S(2)}) copy-start(bf16[128,512]{1,0:T(8,128)(2,1)} %param.41) | copy-start | bytes 393220
  518.9 5.9 copy-start.39
  525.3 6.0 copy-start.30
  4305.2 4.2 copy-start.88
  4305.2 105.2 %all-to-all-start.1 = ((bf16[8,128,512]{2,1,0:T(8,128)(2,1)}), bf16[8,128,512]{2,1,0:T(8,128)(2,1)S(1)}, u32[]{:S(2)}, u32[]{:S(2)}) async-start(bf16[8,128,512]{2,1,0:T(8,128)(2,1)} %bitcast.3454), calls=%async_computation.1 | async-start | bytes 2097152 | tf_op jit(solution)/shard_map/all_to_all | solution.py:195
  4314.0 89.4 %copy-start.21 = (bf16[128,8,512]{2,0,1:T(8,128)(2,1)S(1)}, bf16[128,8,512]{2,0,1:T(8,128)(2,1)}, u32[]{:S(2)}) copy-start(bf16[128,8,512]{2,0,1:T(8,128)(2,1)} %copy-done.20) | copy-start | bytes 3145732
  4314.0 89.4 %copy-start.85 = (f32[512]{0:T(512)S(1)}, f32[512]{0:T(512)}, u32[]{:S(2)}) copy-start(f32[512]{0:T(512)} %param.44) | copy-start | bytes 6148
  4410.4 7.4 copy-start.36
  4410.4 27.7 all-to-all-start.5
  4467.3 20.8 all-to-all-start.3
  4471.7 950.5 %reduce-scatter.2.cloned.1.call-start = ((), (), s32[]{:S(2)}) async-start(), calls=%async_computation.11 | async-start | bytes 103809024 | tf_op jit(solution)/shard_map/reduce_scatter | solution.py:276
  4496.1 13.7 copy-start.28
  4496.1 13.7 copy-start.14
  4601.2 6.6 copy-start.2
  4601.2 856.6 %all-reduce.14.cloned.1.call-start = ((), (), s32[]{:S(2)}) async-start(), calls=%async_computation.13 | async-start | bytes 1179648 | tf_op jit(solution)/shard_map/psum | solution.py:285
  4607.9 13.4 copy-start.15
  4621.3 23.1 copy-start.8
  4621.3 23.1 copy-start.59
  4621.3 23.1 copy-start.78
  4621.3 23.1 copy-start.80
  4644.4 24.7 copy-start.35
  4672.8 15.8 copy-start.29
  4672.8 15.8 copy-start.82
  4688.6 14.8 copy-start.46
  4703.4 38.7 copy-start.44
  4703.4 38.7 copy-start.45
  (54 other events, 133.8 us)
Sparse Core Ops, SparseCore 0:
  9.6 204.2 all-gather.2
  215.4 105.9 all-gather.4
  437.2 81.6 all-reduce.11
  4601.3 820.7 reduce-scatter.1
  5425.3 32.5 all-reduce.13
where the time goes:
time: 5550 us; the launch traced here: 5470 us
  other arithmetic  2700 us (49%)
  waiting for transfers between devices  1150 us (21%)
  local copies, waits for them, and re-layouts  1140 us (21%)
  matrix products  189 us (3%)
  blocking collectives  166 us (3%)
  loops' own time  74.2 us (1%)
    reduce_sum x512, other arithmetic, back_row(): size_grad = jnp.sum(log_grad * rates, axis=0) + shared * row_input  735 us
    reduce_scatter x1, waiting for transfers between devices, shards(): lax.psum_scatter(jnp.concatenate([inner_part, outer_part], axis=1), ('fsd...  679 us
    mul x2048, other arithmetic, back_row(): input_grad = shared * row_size  674 us
    reduce_sum x768, other arithmetic, back_row(): entry_grad = jnp.sum(state_grad * (row_size * row_input)[None, :], axis=1)  560 us
    concatenate x384, local copies, waits for them, and re-layouts, backward_stretch(): lax.scan(back_row, start_carry, (step_sizes, step_input, entry_cols, read...  463 us
    all_gather x1, waiting for transfers between devices, token_group(): lax.all_gather(w_in, 'fsdp', axis=0, tiled=True)  203 us
    reduce_sum x640, other arithmetic, one_row(): return (hidden, jnp.sum(row_readout[:, None] * hidden, axis=0))  203 us
    add x128, other arithmetic, back_row(): decay_total = decay_total + log_grad * row_size[None, :]  151 us

commit v1 on v0

v1 whole, which is shorter than its diff:
```python
from functools import partial

import jax
import jax.numpy as jnp
from jax import lax
from jax.experimental import pallas as pl
from jax.experimental.pallas import tpu as pltpu
from jax.sharding import PartitionSpec as P

EPS = 1e-05
LOG2E = 1.4426950408889634
NT = (((1,), (1,)), ((), ()))
TN = (((0,), (0,)), ((), ()))
ROWS = 128
SUB = 16


def softplus(x):
    e = jnp.exp(-jnp.abs(x))
    return jnp.maximum(x, 0.0) + jnp.log1p(e)


def block_diagonal(columns, states):
    wide = SUB * states
    lane = lax.broadcasted_iota(jnp.int32, (states, wide), 1)
    row = lax.broadcasted_iota(jnp.int32, (states, wide), 0)
    tile = (lax.rem(lane, states) == row).astype(jnp.bfloat16)
    spread = lax.dot_general(columns.astype(jnp.bfloat16), tile, TN, preferred_element_type=jnp.float32)
    block = lax.broadcasted_iota(jnp.int32, (ROWS, wide), 1) // states
    step = lax.rem(lax.broadcasted_iota(jnp.int32, (ROWS, wide), 0), SUB)
    return jnp.where(block == step, spread, 0.0).astype(jnp.bfloat16)


def scan_forward_kernel(
    low_rank, states, lanes,
    sel_ref, u_ref, dtp_ref, bias_ref, alog_ref, skip_ref,
    y_ref, h_ref, delta_ref, sig_ref,
    state, pre, weighted, diag, decay,
):
    chan = u_ref.shape[1]

    @pl.when(pl.program_id(0) == 0)
    def _():
        state[...] = jnp.zeros_like(state)
        decay[...] = -jnp.exp(alog_ref[...]) * LOG2E

    low = sel_ref[:low_rank, :].astype(jnp.bfloat16)
    pre[...] = lax.dot_general(low, dtp_ref[...], TN, preferred_element_type=jnp.float32)
    entry = sel_ref[low_rank : low_rank + states, :]
    diag[...] = block_diagonal(sel_ref[low_rank + states :, :], states)

    def piece(sub, _):
        base = pl.multiple_of(sub * SUB, SUB)
        rows = pl.ds(base, SUB)
        size = pre[rows, :] + bias_ref[...]
        delta = softplus(size)
        delta_ref[rows, :] = delta
        sig_ref[rows, :] = jnp.exp(size - delta).astype(jnp.bfloat16)
        u_float = u_ref[rows, :].astype(jnp.float32)
        weighted[rows, :] = delta * u_float
        cols = pltpu.roll(entry, lax.rem(ROWS - base, ROWS), 1)
        for start in range(0, chan, lanes):
            at = pl.ds(start, lanes)
            rate = decay[:, at]
            hidden = state[:, at]
            for step in range(SUB):
                row = pl.ds(base + step, 1)
                grow = jnp.exp2(delta_ref[row, at] * rate)
                hidden = grow * hidden + cols[:, step : step + 1] * weighted[row, at]
                h_ref[pl.ds(pl.multiple_of((base + step) * states, states), states), at] = hidden.astype(jnp.bfloat16)
            state[:, at] = hidden
            held = h_ref[pl.ds(pl.multiple_of(base * states, SUB * states), SUB * states), at]
            out = jnp.dot(diag[rows, :], held, preferred_element_type=jnp.float32)
            y_ref[rows, at] = (out + skip_ref[:, at] * u_float[:, start : start + lanes]).astype(jnp.bfloat16)
        return 0

    lax.fori_loop(0, ROWS // SUB, piece, 0)


def scan_forward(select, u_act, dt_proj, dt_bias, a_log, d_skip):
    length, chan = u_act.shape
    states = a_log.shape[0]
    low_rank = dt_proj.shape[0]
    lanes = min(256, chan)
    whole = lambda shape: pl.BlockSpec(shape, lambda i: (0, 0))
    by_rows = pl.BlockSpec((ROWS, chan), lambda i: (i, 0))
    return pl.pallas_call(
        partial(scan_forward_kernel, low_rank, states, lanes),
        grid=(length // ROWS,),
        in_specs=[
            pl.BlockSpec((select.shape[0], ROWS), lambda i: (0, i)),
            by_rows,
            whole((low_rank, chan)),
            whole((1, chan)),
            whole((states, chan)),
            whole((1, chan)),
        ],
        out_specs=[by_rows, pl.BlockSpec((ROWS * states, chan), lambda i: (i, 0)), by_rows, by_rows],
        out_shape=[
            jax.ShapeDtypeStruct((length, chan), jnp.bfloat16),
            jax.ShapeDtypeStruct((length * states, chan), jnp.bfloat16),
            jax.ShapeDtypeStruct((length, chan), jnp.float32),
            jax.ShapeDtypeStruct((length, chan), jnp.bfloat16),
        ],
        scratch_shapes=[
            pltpu.VMEM((states, chan), jnp.float32),
            pltpu.VMEM((ROWS, chan), jnp.float32),
            pltpu.VMEM((ROWS, chan), jnp.float32),
            pltpu.VMEM((ROWS, SUB * states), jnp.bfloat16),
            pltpu.VMEM((states, chan), jnp.float32),
        ],
        compiler_params=pltpu.CompilerParams(vmem_limit_bytes=40 * 2**20),
        cost_estimate=pl.CostEstimate(
            flops=12 * length * states * chan,
            bytes_accessed=length * chan * (2 * states + 10),
            transcendentals=length * states * chan,
        ),
        name="scan_forward",
    )(select, u_act, dt_proj, dt_bias.reshape(1, chan), a_log, d_skip.reshape(1, chan))


def scan_backward_kernel(
    low_rank, states, lanes,
    sel_ref, h_ref, before_ref, delta_ref, sig_ref, u_ref, dy_ref, alog_ref, skip_ref,
    pre_ref, upart_ref, ent_ref, rdo_ref, dec_ref, bias_ref, skipg_ref,
    carry, dyf, weighted, diag, decay, rates16, gbuf, abuf, dbuf,
):
    chan = u_ref.shape[1]
    wide = SUB * states
    step_id = pl.program_id(0)
    last = pl.num_programs(0) - 1

    @pl.when(step_id == 0)
    def _():
        carry[...] = jnp.zeros_like(carry)
        rates = -jnp.exp(alog_ref[...])
        decay[...] = rates * LOG2E
        rates16[...] = rates.astype(jnp.bfloat16)
        dec_ref[...] = jnp.zeros_like(dec_ref)
        bias_ref[...] = jnp.zeros_like(bias_ref)
        skipg_ref[...] = jnp.zeros_like(skipg_ref)

    readout = sel_ref[low_rank + states :, :]
    diag[...] = block_diagonal(sel_ref[low_rank : low_rank + states, :], states)
    block = lax.broadcasted_iota(jnp.int32, (SUB, wide), 1) // states
    inside = block == lax.broadcasted_iota(jnp.int32, (SUB, wide), 0)
    ones = jnp.where(inside, 1.0, 0.0).astype(jnp.bfloat16)
    member = lax.rem(lax.broadcasted_iota(jnp.int32, (states, wide), 1), states)
    gather = jnp.where(member == lax.broadcasted_iota(jnp.int32, (states, wide), 0), 1.0, 0.0).astype(jnp.bfloat16)

    def piece(index, _):
        sub = ROWS // SUB - 1 - index
        base = pl.multiple_of(sub * SUB, SUB)
        rows = pl.ds(base, SUB)
        hrows = pl.ds(pl.multiple_of(base * states, wide), wide)
        u_float = u_ref[rows, :].astype(jnp.float32)
        delta = delta_ref[rows, :]
        dy_float = dy_ref[rows, :].astype(jnp.float32)
        dyf[...] = dy_float
        weighted[...] = (delta * u_float).astype(jnp.bfloat16)
        cols = pltpu.roll(readout, lax.rem(ROWS - base, ROWS), 1)
        first = lax.max(base * states - states, 0)
        ent = jnp.zeros((SUB, wide), jnp.float32)
        rdo = jnp.zeros((SUB, wide), jnp.float32)
        for start in range(0, chan, lanes):
            at = pl.ds(start, lanes)
            rate = decay[:, at]
            rate16 = rates16[:, at]
            passed = carry[:, at]
            inner = h_ref[pl.ds(pl.multiple_of(first, states), states), at]
            outer = jnp.where(step_id == last, jnp.zeros_like(inner), before_ref[:, at])
            earliest = jnp.where(sub == 0, outer, inner)
            for step in reversed(range(SUB)):
                row = pl.ds(base + step, 1)
                size = jnp.broadcast_to(delta_ref[row, at], (states, lanes))
                grow = jnp.exp2(size * rate)
                grad = cols[:, step : step + 1] * dyf[pl.ds(step, 1), at] + passed
                passed = grow * grad
                if step:
                    earlier = h_ref[pl.ds(pl.multiple_of((base + step - 1) * states, states), states), at]
                else:
                    earlier = earliest
                logg = passed.astype(jnp.bfloat16) * earlier
                here = pl.ds(step * states, states)
                gbuf[here, at] = grad.astype(jnp.bfloat16)
                abuf[here, at] = logg * rate16
                dbuf[here, at] = logg * size.astype(jnp.bfloat16)
            carry[:, at] = passed
            shared = jnp.dot(diag[rows, :], gbuf[:, at], preferred_element_type=jnp.float32)
            size_a = jnp.dot(ones, abuf[:, at], preferred_element_type=jnp.float32)
            dec_ref[:, at] += jnp.dot(gather, dbuf[:, at], preferred_element_type=jnp.float32)
            rdo += lax.dot_general(dy_ref[rows, at], h_ref[hrows, at], NT, preferred_element_type=jnp.float32)
            ent += lax.dot_general(weighted[:, at], gbuf[:, at], NT, preferred_element_type=jnp.float32)
            u_here = u_float[:, start : start + lanes]
            dy_here = dy_float[:, start : start + lanes]
            pre16 = ((size_a + shared * u_here) * sig_ref[rows, at].astype(jnp.float32)).astype(jnp.bfloat16)
            pre_ref[rows, at] = pre16
            bias_ref[:, at] += jnp.sum(pre16.astype(jnp.float32), axis=0, keepdims=True)
            skipg_ref[:, at] += jnp.sum(dy_here * u_here, axis=0, keepdims=True)
            upart_ref[rows, at] = shared * delta[:, start : start + lanes] + skip_ref[:, at] * dy_here
        ent_ref[pl.ds(sub, 1), :] = jnp.sum(jnp.where(inside, ent, 0.0), axis=0, keepdims=True)
        rdo_ref[pl.ds(sub, 1), :] = jnp.sum(jnp.where(inside, rdo, 0.0), axis=0, keepdims=True)
        return 0

    lax.fori_loop(0, ROWS // SUB, piece, 0)

    @pl.when(step_id == last)
    def _():
        dec_ref[...] = dec_ref[...] * -jnp.exp(alog_ref[...])


def scan_backward(select, hidden, delta, sig, u_act, y_grad, a_log, d_skip, low_rank):
    length, chan = u_act.shape
    states = a_log.shape[0]
    lanes = min(256, chan)
    wide = SUB * states
    count = length // ROWS
    whole = lambda shape: pl.BlockSpec(shape, lambda i: (0, 0))
    by_rows = pl.BlockSpec((ROWS, chan), lambda i: (count - 1 - i, 0))
    flat = pl.BlockSpec((ROWS // SUB, wide), lambda i: (count - 1 - i, 0))
    outs = pl.pallas_call(
        partial(scan_backward_kernel, low_rank, states, lanes),
        grid=(count,),
        in_specs=[
            pl.BlockSpec((select.shape[0], ROWS), lambda i: (0, count - 1 - i)),
            pl.BlockSpec((ROWS * states, chan), lambda i: (count - 1 - i, 0)),
            pl.BlockSpec((states, chan), lambda i: (jnp.maximum((count - 1 - i) * ROWS - 1, 0), 0)),
            by_rows,
            by_rows,
            by_rows,
            by_rows,
            whole((states, chan)),
            whole((1, chan)),
        ],
        out_specs=[by_rows, by_rows, flat, flat, whole((states, chan)), whole((1, chan)), whole((1, chan))],
        out_shape=[
            jax.ShapeDtypeStruct((length, chan), jnp.bfloat16),
            jax.ShapeDtypeStruct((length, chan), jnp.float32),
            jax.ShapeDtypeStruct((length // SUB, wide), jnp.float32),
            jax.ShapeDtypeStruct((length // SUB, wide), jnp.float32),
            jax.ShapeDtypeStruct((states, chan), jnp.float32),
            jax.ShapeDtypeStruct((1, chan), jnp.float32),
            jax.ShapeDtypeStruct((1, chan), jnp.float32),
        ],
        scratch_shapes=[
            pltpu.VMEM((states, chan), jnp.float32),
            pltpu.VMEM((SUB, chan), jnp.float32),
            pltpu.VMEM((SUB, chan), jnp.bfloat16),
            pltpu.VMEM((ROWS, wide), jnp.bfloat16),
            pltpu.VMEM((states, chan), jnp.float32),
            pltpu.VMEM((states, chan), jnp.bfloat16),
            pltpu.VMEM((wide, chan), jnp.bfloat16),
            pltpu.VMEM((wide, chan), jnp.bfloat16),
            pltpu.VMEM((wide, chan), jnp.bfloat16),
        ],
        compiler_params=pltpu.CompilerParams(vmem_limit_bytes=40 * 2**20),
        cost_estimate=pl.CostEstimate(
            flops=30 * length * states * chan,
            bytes_accessed=length * chan * (2 * states + 16),
            transcendentals=length * states * chan,
        ),
        name="scan_backward",
    )(select, hidden, hidden, delta, sig, u_act, y_grad, a_log, d_skip.reshape(1, chan))
    pre_grad, u_part, entry, readout, dec, bias, skip = outs
    return pre_grad, u_part, entry.reshape(length, states), readout.reshape(length, states), dec, bias[0], skip[0]


def silu_slope(values):
    sigmoid_value = jax.nn.sigmoid(values)
    return sigmoid_value * (1.0 + values * (1.0 - sigmoid_value))


def swap(values, axis, size, bit):
    return lax.ppermute(values, axis, [(index, index ^ bit) for index in range(size)])


def orders(size):
    bits = [1 << place for place in range(size.bit_length() - 1)]
    return [bits[turn:] + bits[:turn] for turn in range(len(bits))] or [[]]


def cut(values, count, axis):
    width = values.shape[axis] // count
    return [lax.slice_in_dim(values, at * width, (at + 1) * width, axis=axis) for at in range(count)]


def sum_over_group(values, size, group, axis):
    ways = orders(group)
    done = []
    for part, way in zip(cut(values, len(ways), axis), ways):
        for bit in way:
            part = part + swap(part, "seq", size, bit)
        done.append(part)
    return jnp.concatenate(done, axis=axis)


def gather_tokens(blocks, size, group, place, half):
    rows, width = blocks.shape[1:]
    mine = lax.dynamic_index_in_dim(blocks, half, 0, keepdims=False)
    other = swap(lax.dynamic_index_in_dim(blocks, 1 - half, 0, keepdims=False), "seq", size, group)
    ways = orders(group)
    parts = len(ways)
    buffer = jnp.zeros((size, rows, width), blocks.dtype)
    for source, side in ((mine, half), (other, 1 - half)):
        for at, (part, way) in enumerate(zip(cut(source, parts, 1), ways)):
            held = [(0, part)]
            for bit in way:
                sent = swap(jnp.stack([piece for _, piece in held]), "seq", size, bit)
                held = held + [(offset ^ bit, sent[index]) for index, (offset, _) in enumerate(held)]
            for offset, piece in held:
                where = side * group + (place ^ offset)
                buffer = lax.dynamic_update_slice(buffer, piece[None], (where, 0, at * (width // parts)))
    return buffer


def scatter_tokens(total, size, group, place, half):
    rows, width = total.shape[1:]
    ways = orders(group)
    done = []
    for part, way in zip(cut(total.reshape(2, group, rows, width), len(ways), 3), ways):
        held = [(offset, None) for offset in range(group)]
        part = {offset: lax.dynamic_index_in_dim(part, place ^ offset, 1, keepdims=False) for offset in range(group)}
        for bit in way:
            keep = [offset for offset in part if not offset & bit]
            sent = swap(jnp.stack([part[offset ^ bit] for offset in keep]).astype(jnp.bfloat16), "seq", size, bit)
            part = {offset: part[offset] + sent[index].astype(jnp.float32) for index, offset in enumerate(keep)}
        done.append(part[0])
    both = jnp.concatenate(done, axis=2)
    mine = lax.dynamic_index_in_dim(both, half, 0, keepdims=False)
    other = lax.dynamic_index_in_dim(both, 1 - half, 0, keepdims=False).astype(jnp.bfloat16)
    other = swap(other, "seq", size, group).astype(jnp.float32)
    first = jnp.where(half == 0, mine, other)
    second = jnp.where(half == 0, other, mine)
    return jnp.stack([first, second])


def own_columns(weight, start, cols, place, group):
    return jnp.concatenate(
        [lax.dynamic_slice_in_dim(weight, start + (place + turn * group) * cols, cols, 1) for turn in range(2)], axis=1
    )


def both_blocks(values, size, group, half):
    other = swap(values, "seq", size, group)
    return jnp.concatenate([jnp.where(half == 0, values, other), jnp.where(half == 0, other, values)], axis=-1)


def rows_to_owner(partial_sum, size, group):
    reduced = lax.psum_scatter(partial_sum, "fsdp", scatter_dimension=0, tiled=True)
    rows, cols = reduced.shape
    pieces = lax.all_to_all(reduced.reshape(size, rows // size, cols), "seq", split_axis=0, concat_axis=0, tiled=True)
    pieces = pieces.reshape(2, group, rows // size, 2, cols // 2).astype(jnp.float32)
    summed = pieces[0] + pieces[1]
    return jnp.transpose(summed, (1, 2, 0, 3)).reshape(rows // size, group * cols)


def shards(
    hidden_in,
    cotangent,
    lengths,
    norm_gain,
    w_in,
    conv_w,
    conv_b,
    x_proj,
    dt_proj_w,
    dt_bias,
    a_log,
    d_skip,
    w_out,
):
    size = lax.axis_size("seq")
    group = size // 2
    index = lax.axis_index("seq")
    half, place = index // group, index % group
    rows_dev, width = hidden_in.shape[1:]
    length = size * rows_dev
    cols = conv_b.shape[0]
    inner = w_out.shape[1]
    states, low_rank = a_log.shape[0], dt_proj_w.shape[0]
    taps = conv_w.shape[0]
    bf16, f32 = jnp.bfloat16, jnp.float32

    w_x = lax.all_gather(own_columns(w_in, 0, cols, place, group), "fsdp", axis=0, tiled=True)
    w_z = lax.all_gather(own_columns(w_in, inner, cols, place, group), "fsdp", axis=0, tiled=True)
    w_o = lax.all_gather(own_columns(w_out, 0, cols, place, group), "fsdp", axis=0, tiled=True)

    flat = hidden_in.astype(f32)
    inverse = lax.rsqrt(jnp.mean(flat * flat, axis=-1, keepdims=True) + EPS)
    scaled = flat * inverse
    tokens = gather_tokens((scaled * norm_gain).astype(bf16), size, group, place, half).reshape(length, width)

    small = jnp.concatenate([conv_w, conv_b[None], dt_bias[None], a_log, d_skip[None]], axis=0)
    small = both_blocks(small, size, group, half)
    conv_taps, conv_bias, step_bias = small[:taps], small[taps], small[taps + 1]
    log_rates, skip = small[taps + 2 : taps + 2 + states], small[taps + 2 + states]
    proj = both_blocks(jnp.concatenate([x_proj, dt_proj_w], axis=0), size, group, half)
    sel_proj, size_proj = proj[: x_proj.shape[0]], proj[x_proj.shape[0] :]

    positions = lax.iota(jnp.int32, length)
    valid = (positions < lax.dynamic_index_in_dim(lengths, half, 0, keepdims=False)).astype(f32)[:, None]
    cot = gather_tokens(cotangent, size, group, place, half).reshape(length, width)

    x_part = jnp.dot(tokens, w_x, preferred_element_type=f32).astype(bf16)
    x_float = jnp.pad(x_part.astype(f32), ((taps - 1, 0), (0, 0)))
    pre_conv = conv_bias + sum(conv_taps[at] * x_float[at : at + length] for at in range(taps))
    u_act = jax.nn.silu(pre_conv).astype(bf16)
    select = lax.dot_general(sel_proj, u_act, NT, preferred_element_type=f32)
    select = sum_over_group(select, size, group, 1)
    z_part = jnp.dot(tokens, w_z, preferred_element_type=f32)
    branch_grad = (cot.astype(f32) * valid).astype(bf16)
    gated_grad = jnp.dot(branch_grad, w_o, preferred_element_type=f32)
    z_gate = jax.nn.silu(z_part)
    y_grad = (gated_grad * z_gate).astype(bf16)

    y_sent, held, delta, sig = scan_forward(select, u_act, size_proj, step_bias, log_rates, skip)
    y_float = y_sent.astype(f32)
    gated = (y_float * z_gate).astype(bf16)
    z_grad = (gated_grad * y_float * silu_slope(z_part)).astype(bf16)

    branch = lax.dot_general(gated, w_o, NT, preferred_element_type=f32)
    branch = scatter_tokens(branch.reshape(size, rows_dev, width), size, group, place, half)
    own = index * rows_dev + lax.iota(jnp.int32, rows_dev)
    own_valid = (own[None] < lengths[:, None]).astype(f32)[..., None]
    block_out = (flat + own_valid * branch).astype(bf16)

    out_part = lax.dot_general(branch_grad, gated, TN, preferred_element_type=f32)
    grad_w_out = rows_to_owner(out_part, size, group)
    z_term = lax.dot_general(tokens, z_grad, TN, preferred_element_type=f32)
    grad_w_z = rows_to_owner(z_term, size, group)

    pre_grad, u_part, entry, readout, log_grad, bias_grad, skip_grad = scan_backward(
        select, held, delta, sig, u_act, y_grad, log_rates, skip, low_rank
    )
    low_grad = lax.dot_general(size_proj, pre_grad, NT, preferred_element_type=f32)
    select_part = jnp.concatenate([low_grad, entry.T, readout.T], axis=0)
    select_grad = sum_over_group(select_part, size, group, 1).astype(bf16)
    proj_grad = jnp.dot(select[:low_rank].astype(bf16), pre_grad, preferred_element_type=f32)
    sel_grad = jnp.dot(select_grad, u_act, preferred_element_type=f32)

    u_grad = u_part + lax.dot_general(select_grad, sel_proj, TN, preferred_element_type=f32)
    conv_grad = u_grad * silu_slope(pre_conv)
    convb_grad = jnp.sum(conv_grad, axis=0)
    convw_grad = jnp.stack([jnp.sum(conv_grad * x_float[at : at + length], axis=0) for at in range(taps)])
    late = jnp.pad(conv_grad, ((0, taps - 1), (0, 0)))
    x_grad = sum(conv_taps[at] * late[taps - 1 - at : taps - 1 - at + length] for at in range(taps)).astype(bf16)

    normed_grad = lax.dot_general(x_grad, w_x, NT, preferred_element_type=f32)
    normed_grad = normed_grad + lax.dot_general(z_grad, w_z, NT, preferred_element_type=f32)
    normed_grad = scatter_tokens(normed_grad.reshape(size, rows_dev, width), size, group, place, half)
    scaled_grad = normed_grad * norm_gain
    grad_in = cotangent.astype(f32) + inverse * (
        scaled_grad - scaled * jnp.mean(scaled_grad * scaled, axis=-1, keepdims=True)
    )

    x_term = lax.dot_general(tokens, x_grad, TN, preferred_element_type=f32)
    grad_w_x = rows_to_owner(x_term, size, group)
    gain_part = jnp.sum(w_x.astype(f32) * x_term, axis=1) + jnp.sum(w_z.astype(f32) * z_term, axis=1)
    grad_gain = lax.psum(gain_part, ("fsdp", "seq")) / norm_gain

    stacked = jnp.concatenate(
        [convw_grad, convb_grad[None], sel_grad, proj_grad, bias_grad[None], log_grad, skip_grad[None]], axis=0
    )
    mine = lax.dynamic_slice_in_dim(stacked, half * cols, cols, 1)
    other = swap(lax.dynamic_slice_in_dim(stacked, (1 - half) * cols, cols, 1), "seq", size, group)
    stacked = lax.psum(mine + other, "fsdp")
    pieces = []
    at = 0
    for count in (taps, 1, x_proj.shape[0], low_rank, 1, states, 1):
        pieces.append(stacked[at : at + count])
        at += count
    convw, convb, xproj, dtproj, dtbias, alog, dskip = pieces
    return (
        block_out,
        grad_in.astype(bf16),
        grad_gain,
        jnp.concatenate([grad_w_x, grad_w_z], axis=1),
        convw,
        convb[0],
        xproj,
        dtproj,
        dtbias[0],
        alog,
        dskip[0],
        grad_w_out,
    )


def solution(mesh):
    return jax.shard_map(
        shards,
        mesh=mesh,
        in_specs=(
            P("fsdp", "seq", None),
            P("fsdp", "seq", None),
            P("fsdp"),
            P(),
            P("fsdp", None),
            P(None, "seq"),
            P("seq"),
            P(None, "seq"),
            P(None, "seq"),
            P("seq"),
            P(None, "seq"),
            P("seq"),
            P("fsdp", None),
        ),
        out_specs=(
            P("fsdp", "seq", None),
            P("fsdp", "seq", None),
            P(),
            P(("fsdp", "seq"), None),
            P(None, "seq"),
            P("seq"),
            P(None, "seq"),
            P(None, "seq"),
            P("seq"),
            P(None, "seq"),
            P("seq"),
            P(("fsdp", "seq"), None),
        ),
        check_vma=False,
    )
```

time: 5550 us -> 668 us (0.12); the launches traced: 5470 us -> 661 us
  other arithmetic: 2700 us -> 63.9 us
  local copies, waits for them, and re-layouts: 1140 us -> 80.5 us
  waiting for transfers between devices: 1150 us -> 161 us
  Pallas kernels: 0 us -> 102 us
  matrix products: 189 us -> 90.9 us
  blocking collectives: 166 us -> 79.1 us
  loops' own time: 74.2 us -> 0 us
    reduce_sum x2695 -> x3, other arithmetic: 1670 us -> 5.9 us  [the longest x1 5.11 us: shards(): jnp.sum(conv_grad * x_float[at:at + length], axis=0)]
    mul x8192 -> x0, other arithmetic: 703 us -> none  [the longest x2048 674 us: back_row(): input_grad = shared * row_size]
    reduce_scatter x1 -> x3, waiting for transfers between devices: 679 us -> 0.04 us  [rows_to_owner(): lax.psum_scatter(partial_sum, 'fsdp', scatter_dimension=0, tiled=True)]
    concatenate x640 -> x3, local copies, waits for them, and re-layouts: 568 us -> 3.63 us  [the longest x1 2.79 us: shards(): jnp.concatenate([convw_grad, convb_grad[None], sel_grad, proj_grad, bias_...]
    all_gather x2 -> x3, waiting for transfers between devices: 286 us -> 0.02 us  [the longest x1 0.02 us: shards(): lax.all_gather(own_columns(w_out, 0, cols, place, group), 'fsdp', axis=0,...]
    mul x513 -> x0, local copies, waits for them, and re-layouts: 167 us -> none  [the longest x128 139 us: one_row(): row_entry[:, None] * (row_size * row_input)[None, :]]
    dynamic_update_slice x680 -> x31, local copies, waits for them, and re-layouts: 187 us -> 23.2 us  [gather_tokens(): lax.dynamic_update_slice(buffer, piece[None], (where, 0, at * (width // p...]
    ppermute x0 -> x39, waiting for transfers between devices: none -> 148 us  [swap(): lax.ppermute(values, axis, [(index, index ^ bit) for index in range(size)])]
where the time goes in v1:
time: 668 us; the launch traced here: 661 us
  waiting for transfers between devices  161 us (24%)
  Pallas kernels  102 us (15%)
  matrix products  90.9 us (14%)
  local copies, waits for them, and re-layouts  80.5 us (12%)
  blocking collectives  79.1 us (12%)
  starting transfers between devices  68.5 us (10%)
  other arithmetic  63.9 us (10%)
  between operations  15.5 us (2%)
    ppermute x39, waiting for transfers between devices, swap(): lax.ppermute(values, axis, [(index, index ^ bit) for index in range(size)])  148 us
    psum x1, blocking collectives, shards(): grad_gain = lax.psum(gain_part, ('fsdp', 'seq')) / norm_gain  79.1 us
    pallas_call x1, Pallas kernels, scan_backward(): pl.pallas_call(partial(scan_backward_kernel, low_rank, states, lanes), gr...  62.1 us
    ppermute x39, starting transfers between devices, swap(): lax.ppermute(values, axis, [(index, index ^ bit) for index in range(size)])  52.3 us
    pallas_call x1, Pallas kernels, scan_forward(): pl.pallas_call(partial(scan_forward_kernel, low_rank, states, lanes), gri...  39.7 us
    dynamic_update_slice x31, local copies, waits for them, and re-layouts, gather_tokens(): lax.dynamic_update_slice(buffer, piece[None], (where, 0, at * (width // p...  23.2 us
    unnamed x121, local copies, waits for them, and re-layouts  15.5 us
    all_to_all x3, starting transfers between devices, rows_to_owner(): lax.all_to_all(reduced.reshape(size, rows // size, cols), 'seq', split_ax...  15.4 us
  transfers between devices with their start and end apart: 49, of which 22 were waited for; matrix products, arithmetic and copies ran while one was open for 32% of the time, Pallas kernels for 15%

profile of v1, /device:TPU:0, one launch (start us, length us, event | category | flops | bytes accessed | tf_op | source)
XLA Modules:
  0.0 661.1 jit_solution(17141602328177918840)
XLA Ops:
  14.4 2.9 collective-permute-start.2
  20.5 2.6 collective-permute-start.6
  26.2 2.6 broadcast.61.clone.1
  29.5 2.5 broadcast.61.clone
  35.9 11.9 %collective-permute-done.1 = f32[23,512]{1,0:T(8,128)S(1)} collective-permute-done((f32[23,512]{1,0:T(8,128)S(1)}, f32[23,512]{1,0:T(8,128)S(1)}, u32[]{:S(2)}, u32[]{:S(2)}) %collective-permute-start.1) | collective-permute-done | bytes 47136 | tf_op jit(solution)/shard_map/ppermute | solution.py:274
  48.5 3.0 collective-permute-start.22
  57.1 6.3 collective-permute-done.22
  63.7 7.9 %collective-permute-done = bf16[288,512]{1,0:T(8,128)(2,1)S(1)} collective-permute-done((bf16[288,512]{1,0:T(8,128)(2,1)}, bf16[288,512]{1,0:T(8,128)(2,1)S(1)}, u32[]{:S(2)}, u32[]{:S(2)}) %collective-permute-start) | collective-permute-done | bytes 294944 | tf_op jit(solution)/shard_map/ppermute | solution.py:274
  74.8 9.9 %collective-permute-done.24 = bf16[128,2048]{1,0:T(8,128)(2,1)S(1)} collective-permute-done((bf16[128,2048]{1,0:T(8,128)(2,1)}, bf16[128,2048]{1,0:T(8,128)(2,1)S(1)}, u32[]{:S(2)}, u32[]{:S(2)}) %collective-permute-start.24) | collective-permute-done | bytes 524320 | tf_op jit(solution)/shard_map/ppermute | solution.py:274
  86.9 11.2 %collective-permute-done.21 = bf16[2,128,1024]{2,1,0:T(8,128)(2,1)S(1)} collective-permute-done((bf16[2,128,1024]{2,1,0:T(8,128)(2,1)S(1)}, bf16[2,128,1024]{2,1,0:T(8,128)(2,1)S(1)}, u32[]{:S(2)}, u32[]{:S(2)}) %collective-permute-start.21) | collective-permute-done | bytes 524320 | tf_op jit(solution)/shard_map/ppermute | solution.py:274
  109.9 2.6 collective-permute-done.27
  126.0 5.6 collective-permute-done.26
  138.4 7.8 %convert_convert_fusion = f32[1024,1024]{1,0:T(8,128)S(1)} fusion(bf16[1024,2048]{1,0:T(8,128)(2,1)} %bitcast.11, bf16[2048,1024]{0,1:T(8,128)(2,1)} %all-gather.4.cloned.1.call-done), kind=kOutput, calls=%fused_computation.51 | convolution fusion | flops 4297064448 | bytes 12582912 | tf_op jit(solution)/shard_map/dot_general | solution.py:404
  146.2 4.1 multiply_convert_fusion.1
  153.0 4.9 fusion
  158.3 3.0 collective-permute-done.13
  162.4 7.6 %fusion.71 = f32[1024,1024]{1,0:T(8,128)S(1)} fusion(bf16[1024,2048]{1,0:T(8,128)(2,1)} %bitcast.11, bf16[2048,1024]{0,1:T(8,128)(2,1)} %all-gather.6.cloned.1.call-done), kind=kOutput, calls=%fused_computation.230 | convolution fusion | flops 4294967296 | bytes 12582912 | tf_op jit(solution)/shard_map/dot_general | solution.py:410
  172.2 39.7 %scan_forward.1 = (bf16[1024,1024]{1,0:T(8,128)(2,1)S(1)}, bf16[16384,1024]{1,0:T(8,128)(2,1)}, f32[1024,1024]{1,0:T(8,128)S(1)}, bf16[1024,1024]{1,0:T(8,128)(2,1)S(1)}) custom-call(f32[160,1024]{1,0:T(8,128)S(1)} %pad_maximum_fusion.8.sel_ref, bf16[1024,1024]{1,0:T(8,128)(2,1)S(1)} %get-tuple-element.40.u_ref, ...), custom_call_target="tpu_custom_call" | custom-call | flops 201326592 | bytes 44040192 | tf_op jit(solution)/shard_map/scan_forward/pallas_call | solution.py:87
  216.8 7.0 %fusion.62 = f32[2048,1024]{1,0:T(8,128)} fusion(bf16[1024,2048]{1,0:T(8,128)(2,1)S(1)} %copy-done.24, bf16[1024,1024]{1,0:T(8,128)(2,1)S(1)} %get-tuple-element.23, f32[1024,1024]{1,0:T(8,128)S(1)} %fusion.71), kind=kOutput, calls=%fused_computation.223 | convolution fusion | flops 4302307328 | bytes 18874368 | tf_op jit(solution)/shard_map/dot_general | solution.py:427
  224.1 12.9 %fusion.3 = (bf16[1024,1024]{1,0:T(8,128)(2,1)S(1)}, bf16[1024,1024]{1,0:T(8,128)(2,1)}) fusion(bf16[1024,1024]{1,0:T(8,128)(2,1)} %copy-done.8, f32[1024,1024]{1,0:T(8,128)} %copy-done.57, bf16[1024,2048]{1,0:T(8,128)(2,1)} %fusion, bf16[2048,1024]{1,0:T(8,128)(2,1)} %all-gather.8.cloned.1.call-done), kind=kOutput, calls=%fused_computation.8 | convolution fusion | flops 4309647360 | bytes 18874368 | tf_op jit(solution)/shard_map/dot_general | solution.py:412
  237.0 10.4 %multiply_reduce_fusion = (f32[2048]{0:T(1024)S(1)}, f32[2048,1024]{0,1:T(8,128)}) fusion(bf16[2048,1024]{0,1:T(8,128)(2,1)S(1)} %copy-done.53, bf16[1024,2048]{1,0:T(8,128)(2,1)} %bitcast.11, bf16[1024,1024]{1,0:T(8,128)(2,1)S(1)} %get-tuple-element.44), kind=kOutput, calls=%fused_computation.2 | convolution fusion | flops 4301256704 | bytes 18882560 | tf_op jit(solution)/shard_map/dot_general | solution.py:429
  251.0 62.1 %scan_backward.1 = (bf16[1024,1024]{1,0:T(8,128)(2,1)S(1)}, f32[1024,1024]{1,0:T(8,128)S(1)}, f32[64,256]{1,0:T(8,128)S(1)}, f32[64,256]{1,0:T(8,128)S(1)}, f32[...) custom-call(f32[160,1024]{1,0:T(8,128)S(1)} %pad_maximum_fusion.8.sel_ref, ...), custom_call_target="tpu_custom_call" | custom-call | flops 503316480 | bytes 50331648 | tf_op jit(solution)/shard_map/scan_backward/pallas_call | solution.py:221
  317.3 2.6 fusion.72
  323.1 5.1 collective-permute-done.29
  328.2 3.6 collective-permute-done.31
  333.8 5.2 collective-permute-done.30
  340.6 2.8 fusion.53
  343.4 5.1 multiply_reduce_fusion.2
  350.7 10.2 %multiply_reduce_fusion.1 = (f32[2048]{0:T(1024)S(1)}, f32[2048,1024]{0,1:T(8,128)}) fusion(bf16[2048,1024]{0,1:T(8,128)(2,1)S(1)} %copy-done.54, bf16[1024,2048]{1,0:T(8,128)(2,1)} %bitcast.11, bf16[1024,1024]{1,0:T(8,128)(2,1)S(1)} %add_convert_fusion), kind=kOutput, calls=%fused_computation.3 | convolution fusion | flops 4301256704 | bytes 18882560 | tf_op jit(solution)/shard_map/dot_general | solution.py:456
  361.0 4.5 all-to-all-start.2
  365.5 8.0 %fusion.64 = f32[1024,2048]{1,0:T(8,128)S(1)} fusion(bf16[2048,1024]{1,0:T(8,128)(2,1)} %all-gather.8.cloned.1.call-done, bf16[1024,1024]{1,0:T(8,128)(2,1)} %copy-done.8, f32[1024,1024]{1,0:T(8,128)} %copy-done.57), kind=kOutput, calls=%fused_computation.224 | convolution fusion | flops 4302307328 | bytes 18874368 | tf_op jit(solution)/shard_map/dot_general | solution.py:421
  383.9 2.8 concatenate.56
  389.9 10.7 %fusion.73 = f32[1024,2048]{1,0:T(8,128)} fusion(bf16[1024,1024]{1,0:T(8,128)(2,1)} %copy-done.31, bf16[2048,1024]{0,1:T(8,128)(2,1)} %all-gather.4.cloned.1.call-done), kind=kOutput, calls=%fused_computation.232 | convolution fusion | flops 4294967296 | bytes 14680064 | tf_op jit(solution)/shard_map/dot_general | solution.py:448
  400.5 3.0 copy.50
  403.5 12.3 %all-to-all-done.2 = f32[8,64,1024]{2,1,0:T(8,128)} async-done(((f32[8,64,1024]{2,1,0:T(8,128)}), f32[8,64,1024]{2,1,0:T(8,128)}, u32[]{:S(2)}, u32[]{:S(2)}) %all-to-all-start.2) | async-done | bytes 2097184 | tf_op jit(solution)/shard_map/all_to_all | solution.py:351
  415.8 4.4 all-to-all-start.1
  420.3 8.5 %convolution_add_fusion = f32[1024,2048]{1,0:T(8,128)S(1)} fusion(f32[1024,2048]{1,0:T(8,128)} %fusion.73, bf16[1024,1024]{1,0:T(8,128)(2,1)S(1)} %copy-done.56, bf16[2048,1024]{0,1:T(8,128)(2,1)} %all-gather.6.cloned.1.call-done), kind=kOutput, calls=%fused_computation.25 | convolution fusion | flops 4297064448 | bytes 23068672 | tf_op jit(solution)/shard_map/dot_general | solution.py:449
  439.4 79.1 %psum.14 = f32[2048]{0:T(1024)S(1)} all-reduce(f32[2048]{0:T(1024)S(1)} %add.424), channel_id=1, replica_groups=mesh['fsdp'=4,'seq'=8] {'fsdp','seq'}, use_global_device_ids=true, to_apply=%region_4.5 | all-reduce | flops 2048 | bytes 16384 | tf_op jit(solution)/shard_map/psum | solution.py:459
  519.1 2.3 fusion.33
  527.5 2.6 fusion.31
  531.6 2.6 fusion.29
  536.4 2.9 copy.48
  539.3 6.5 all-to-all-start
  546.6 2.9 collective-permute-start.19
  551.3 3.9 collective-permute-done.36
  558.6 3.8 collective-permute-start.37
  570.0 58.1 %collective-permute-done.19 = bf16[128,2048]{1,0:T(8,128)(2,1)} collective-permute-done((bf16[128,2048]{1,0:T(8,128)(2,1)}, bf16[128,2048]{1,0:T(8,128)(2,1)}, u32[]{:S(2)}, u32[]{:S(2)}) %collective-permute-start.19) | collective-permute-done | bytes 524320 | tf_op jit(solution)/shard_map/ppermute | solution.py:274
  629.5 6.1 collective-permute-done.37
  (329 shorter events, 157.6 us)
Async XLA Ops:
  7.2 131.2 %all-gather.4.cloned.1.call-start = ((), (), s32[]{:S(2)}) async-start(), calls=%async_computation.6 | async-start | bytes 5242880 | tf_op jit(solution)/shard_map/all_gather | solution.py:384
  10.5 152.0 %all-gather.6.cloned.1.call-start = ((), (), s32[]{:S(2)}) async-start(), calls=%async_computation.7 | async-start | bytes 5242880 | tf_op jit(solution)/shard_map/all_gather | solution.py:385
  12.0 212.0 %all-gather.8.cloned.1.call-start = ((), (), s32[]{:S(2)}) async-start(), calls=%async_computation.8 | async-start | bytes 5242880 | tf_op jit(solution)/shard_map/all_gather | solution.py:386
  14.4 34.0 %collective-permute-start.2 = (bf16[1,128,1024]{2,1,0:T(8,128)(2,1)}, bf16[1,128,1024]{2,1,0:T(8,128)(2,1)S(1)}, u32[]{:S(2)}, u32[]{:S(2)}) collective-permute-start(bf16[1,128,1024]{2,1,0:T(8,128)(2,1)} %get-tuple-element.92), channel_id=1, source_target_pairs={{0,1},{1,0},{2,3},{3,2},{4,5},{5,4},{6,7},{7,6},{8,9},{9,8},{10,11... | collective-permute-start | bytes 786440 | tf_op jit(solution)/shard_map/ppermute | solution.py:274
  18.3 34.2 %collective-permute-start.20 = (bf16[1,128,1024]{2,1,0:T(8,128)(2,1)S(1)}, bf16[1,128,1024]{2,1,0:T(8,128)(2,1)S(1)}, u32[]{:S(2)}, u32[]{:S(2)}) collective-permute-start(bf16[1,128,1024]{2,1,0:T(8,128)(2,1)S(1)} %get-tuple-element.88), channel_id=1, source_target_pairs={{0,1},{1,0},{2,3},{3,2},{4,5},{5,4},{6,7},{7,6},{8,9},{9,8},{10,11... | collective-permute-start | bytes 786440 | tf_op jit(solution)/shard_map/ppermute | solution.py:274
  18.4 35.2 %collective-permute-start.4 = (bf16[1,128,1024]{2,1,0:T(8,128)(2,1)S(1)}, bf16[1,128,1024]{2,1,0:T(8,128)(2,1)S(1)}, u32[]{:S(2)}, u32[]{:S(2)}) collective-permute-start(bf16[1,128,1024]{2,1,0:T(8,128)(2,1)S(1)} %get-tuple-element.91), channel_id=1, source_target_pairs={{0,2},{1,3},{2,0},{3,1},{4,6},{5,7},{6,4},{7,5},{8,10},{9,11},{10,... | collective-permute-start | bytes 786440 | tf_op jit(solution)/shard_map/ppermute | solution.py:274
  20.5 53.7 %collective-permute-start.6 = (bf16[128,2048]{1,0:T(8,128)(2,1)}, bf16[128,2048]{1,0:T(8,128)(2,1)S(1)}, u32[]{:S(2)}, u32[]{:S(2)}) collective-permute-start(bf16[128,2048]{1,0:T(8,128)(2,1)} %get-tuple-element.70), channel_id=1, source_target_pairs={{0,4},{1,5},{2,6},{3,7},{4,0},{5,1},{6,2},{7,3},{8,12},{9,13},{10,... | collective-permute-start | bytes 1572872 | tf_op jit(solution)/shard_map/ppermute | solution.py:274
  23.3 24.5 %collective-permute-start.1 = (f32[23,512]{1,0:T(8,128)S(1)}, f32[23,512]{1,0:T(8,128)S(1)}, u32[]{:S(2)}, u32[]{:S(2)}) collective-permute-start(f32[23,512]{1,0:T(8,128)S(1)} %concatenate.45), channel_id=1, source_target_pairs={{0,4},{1,5},{2,6},{3,7},{4,0},{5,1},{6,2},{7,3},{8,12},{9,13},{10,... | collective-permute-start | bytes 141320 | tf_op jit(solution)/shard_map/ppermute | solution.py:274
  26.1 334.9 %reduce-scatter.8.cloned.1.call-start = ((), (), s32[]{:S(2)}) async-start(), calls=%async_computation.12 | async-start | bytes 10485760 | tf_op jit(solution)/shard_map/reduce_scatter | solution.py:349
  47.8 23.8 %collective-permute-start = (bf16[288,512]{1,0:T(8,128)(2,1)}, bf16[288,512]{1,0:T(8,128)(2,1)S(1)}, u32[]{:S(2)}, u32[]{:S(2)}) collective-permute-start(bf16[288,512]{1,0:T(8,128)(2,1)} %constant_dynamic-update-slice_fusion.16), channel_id=1, source_target_pairs={{0,4},{1,5},{2,6},{3,7},{4,0},{5,1},{6,2},{7,3},{8,12},{9,13},{10,... | collective-permute-start | bytes 884744 | tf_op jit(solution)/shard_map/ppermute | solution.py:274
  48.5 14.9 %collective-permute-start.22 = (bf16[1,128,1024]{2,1,0:T(8,128)(2,1)S(1)}, bf16[1,128,1024]{2,1,0:T(8,128)(2,1)S(1)}, u32[]{:S(2)}, u32[]{:S(2)}) collective-permute-start(bf16[1,128,1024]{2,1,0:T(8,128)(2,1)S(1)} %get-tuple-element.87), channel_id=1, source_target_pairs={{0,2},{1,3},{2,0},{3,1},{4,6},{5,7},{6,4},{7,5},{8,10},{9,11},{10,... | collective-permute-start | bytes 786440 | tf_op jit(solution)/shard_map/ppermute | solution.py:274
  52.5 32.2 %collective-permute-start.24 = (bf16[128,2048]{1,0:T(8,128)(2,1)}, bf16[128,2048]{1,0:T(8,128)(2,1)S(1)}, u32[]{:S(2)}, u32[]{:S(2)}) collective-permute-start(bf16[128,2048]{1,0:T(8,128)(2,1)} %get-tuple-element.68), channel_id=1, source_target_pairs={{0,4},{1,5},{2,6},{3,7},{4,0},{5,1},{6,2},{7,3},{8,12},{9,13},{10,... | collective-permute-start | bytes 1572872 | tf_op jit(solution)/shard_map/ppermute | solution.py:274
  53.6 33.2 %collective-permute-start.3 = (bf16[2,128,1024]{2,1,0:T(8,128)(2,1)S(1)}, bf16[2,128,1024]{2,1,0:T(8,128)(2,1)S(1)}, u32[]{:S(2)}, u32[]{:S(2)}) collective-permute-start(bf16[2,128,1024]{2,1,0:T(8,128)(2,1)S(1)} %pad_maximum_fusion.10), channel_id=1, source_target_pairs={{0,2},{1,3},{2,0},{3,1},{4,6},{5,7},{6,4},{7,5},{8,10},{9,11},{10,... | collective-permute-start | bytes 1572872 | tf_op jit(solution)/shard_map/ppermute | solution.py:274
  63.4 34.7 %collective-permute-start.21 = (bf16[2,128,1024]{2,1,0:T(8,128)(2,1)S(1)}, bf16[2,128,1024]{2,1,0:T(8,128)(2,1)S(1)}, u32[]{:S(2)}, u32[]{:S(2)}) collective-permute-start(bf16[2,128,1024]{2,1,0:T(8,128)(2,1)S(1)} %pad_maximum_fusion.14), channel_id=1, source_target_pairs={{0,2},{1,3},{2,0},{3,1},{4,6},{5,7},{6,4},{7,5},{8,10},{9,11},{10,... | collective-permute-start | bytes 1572872 | tf_op jit(solution)/shard_map/ppermute | solution.py:274
  71.6 42.5 %collective-permute-start.5 = (bf16[2,128,1024]{2,1,0:T(8,128)(2,1)S(1)}, bf16[2,128,1024]{2,1,0:T(8,128)(2,1)S(1)}, u32[]{:S(2)}, u32[]{:S(2)}) collective-permute-start(bf16[2,128,1024]{2,1,0:T(8,128)(2,1)S(1)} %pad_maximum_fusion.11), channel_id=1, source_target_pairs={{0,1},{1,0},{2,3},{3,2},{4,5},{5,4},{6,7},{7,6},{8,9},{9,8},{10,11... | collective-permute-start | bytes 1572872 | tf_op jit(solution)/shard_map/ppermute | solution.py:274
  74.1 42.9 %collective-permute-start.23 = (bf16[2,128,1024]{2,1,0:T(8,128)(2,1)S(1)}, bf16[2,128,1024]{2,1,0:T(8,128)(2,1)S(1)}, u32[]{:S(2)}, u32[]{:S(2)}) collective-permute-start(bf16[2,128,1024]{2,1,0:T(8,128)(2,1)S(1)} %pad_maximum_fusion.15), channel_id=1, source_target_pairs={{0,1},{1,0},{2,3},{3,2},{4,5},{5,4},{6,7},{7,6},{8,9},{9,8},{10,11... | collective-permute-start | bytes 1572872 | tf_op jit(solution)/shard_map/ppermute | solution.py:274
  84.7 18.6 %collective-permute-start.7 = (bf16[1,128,1024]{2,1,0:T(8,128)(2,1)S(1)}, bf16[1,128,1024]{2,1,0:T(8,128)(2,1)S(1)}, u32[]{:S(2)}, u32[]{:S(2)}) collective-permute-start(bf16[1,128,1024]{2,1,0:T(8,128)(2,1)S(1)} %get-tuple-element.90), channel_id=1, source_target_pairs={{0,1},{1,0},{2,3},{3,2},{4,5},{5,4},{6,7},{7,6},{8,9},{9,8},{10,11... | collective-permute-start | bytes 786440 | tf_op jit(solution)/shard_map/ppermute | solution.py:274
  86.8 16.5 %collective-permute-start.9 = (bf16[1,128,1024]{2,1,0:T(8,128)(2,1)S(1)}, bf16[1,128,1024]{2,1,0:T(8,128)(2,1)S(1)}, u32[]{:S(2)}, u32[]{:S(2)}) collective-permute-start(bf16[1,128,1024]{2,1,0:T(8,128)(2,1)S(1)} %get-tuple-element.89), channel_id=1, source_target_pairs={{0,2},{1,3},{2,0},{3,1},{4,6},{5,7},{6,4},{7,5},{8,10},{9,11},{10,... | collective-permute-start | bytes 786440 | tf_op jit(solution)/shard_map/ppermute | solution.py:274
  98.1 9.5 %collective-permute-start.25 = (bf16[1,128,1024]{2,1,0:T(8,128)(2,1)S(1)}, bf16[1,128,1024]{2,1,0:T(8,128)(2,1)S(1)}, u32[]{:S(2)}, u32[]{:S(2)}) collective-permute-start(bf16[1,128,1024]{2,1,0:T(8,128)(2,1)S(1)} %get-tuple-element.86), channel_id=1, source_target_pairs={{0,1},{1,0},{2,3},{3,2},{4,5},{5,4},{6,7},{7,6},{8,9},{9,8},{10,11... | collective-permute-start | bytes 786440 | tf_op jit(solution)/shard_map/ppermute | solution.py:274
  103.3 9.2 %collective-permute-start.27 = (bf16[1,128,1024]{2,1,0:T(8,128)(2,1)S(1)}, bf16[1,128,1024]{2,1,0:T(8,128)(2,1)S(1)}, u32[]{:S(2)}, u32[]{:S(2)}) collective-permute-start(bf16[1,128,1024]{2,1,0:T(8,128)(2,1)S(1)} %get-tuple-element.85), channel_id=1, source_target_pairs={{0,2},{1,3},{2,0},{3,1},{4,6},{5,7},{6,4},{7,5},{8,10},{9,11},{10,... | collective-permute-start | bytes 786440 | tf_op jit(solution)/shard_map/ppermute | solution.py:274
  103.3 20.4 %collective-permute-start.8 = (bf16[2,128,1024]{2,1,0:T(8,128)(2,1)S(1)}, bf16[2,128,1024]{2,1,0:T(8,128)(2,1)S(1)}, u32[]{:S(2)}, u32[]{:S(2)}) collective-permute-start(bf16[2,128,1024]{2,1,0:T(8,128)(2,1)S(1)} %pad_maximum_fusion.12), channel_id=1, source_target_pairs={{0,2},{1,3},{2,0},{3,1},{4,6},{5,7},{6,4},{7,5},{8,10},{9,11},{10,... | collective-permute-start | bytes 1572872 | tf_op jit(solution)/shard_map/ppermute | solution.py:274
  107.6 27.7 %collective-permute-start.10 = (bf16[2,128,1024]{2,1,0:T(8,128)(2,1)S(1)}, bf16[2,128,1024]{2,1,0:T(8,128)(2,1)S(1)}, u32[]{:S(2)}, u32[]{:S(2)}) collective-permute-start(bf16[2,128,1024]{2,1,0:T(8,128)(2,1)S(1)} %pad_maximum_fusion.13), channel_id=1, source_target_pairs={{0,1},{1,0},{2,3},{3,2},{4,5},{5,4},{6,7},{7,6},{8,9},{9,8},{10,11... | collective-permute-start | bytes 1572872 | tf_op jit(solution)/shard_map/ppermute | solution.py:274
  112.5 19.1 %collective-permute-start.26 = (bf16[2,128,1024]{2,1,0:T(8,128)(2,1)S(1)}, bf16[2,128,1024]{2,1,0:T(8,128)(2,1)S(1)}, u32[]{:S(2)}, u32[]{:S(2)}) collective-permute-start(bf16[2,128,1024]{2,1,0:T(8,128)(2,1)S(1)} %pad_maximum_fusion.16), channel_id=1, source_target_pairs={{0,2},{1,3},{2,0},{3,1},{4,6},{5,7},{6,4},{7,5},{8,10},{9,11},{10,... | collective-permute-start | bytes 1572872 | tf_op jit(solution)/shard_map/ppermute | solution.py:274
  114.1 22.8 %collective-permute-start.28 = (bf16[2,128,1024]{2,1,0:T(8,128)(2,1)S(1)}, bf16[2,128,1024]{2,1,0:T(8,128)(2,1)S(1)}, u32[]{:S(2)}, u32[]{:S(2)}) collective-permute-start(bf16[2,128,1024]{2,1,0:T(8,128)(2,1)S(1)} %pad_maximum_fusion.17), channel_id=1, source_target_pairs={{0,1},{1,0},{2,3},{3,2},{4,5},{5,4},{6,7},{7,6},{8,9},{9,8},{10,11... | collective-permute-start | bytes 1572872 | tf_op jit(solution)/shard_map/ppermute | solution.py:274
  151.2 7.1 %collective-permute-start.11 = (f32[160,512]{1,0:T(8,128)S(1)}, f32[160,512]{1,0:T(8,128)S(1)}, u32[]{:S(2)}, u32[]{:S(2)}) collective-permute-start(f32[160,512]{1,0:T(8,128)S(1)} %get-tuple-element.78), channel_id=1, source_target_pairs={{0,1},{1,0},{2,3},{3,2},{4,5},{5,4},{6,7},{7,6},{8,9},{9,8},{10,11... | collective-permute-start | bytes 983048 | tf_op jit(solution)/shard_map/ppermute | solution.py:274
  152.7 8.6 %collective-permute-start.13 = (f32[160,512]{1,0:T(8,128)S(1)}, f32[160,512]{1,0:T(8,128)S(1)}, u32[]{:S(2)}, u32[]{:S(2)}) collective-permute-start(f32[160,512]{1,0:T(8,128)S(1)} %get-tuple-element.79), channel_id=1, source_target_pairs={{0,2},{1,3},{2,0},{3,1},{4,6},{5,7},{6,4},{7,5},{8,10},{9,11},{10,... | collective-permute-start | bytes 983048 | tf_op jit(solution)/shard_map/ppermute | solution.py:274
  161.5 8.6 %collective-permute-start.12 = (f32[160,512]{1,0:T(8,128)S(1)}, f32[160,512]{1,0:T(8,128)}, u32[]{:S(2)}, u32[]{:S(2)}) collective-permute-start(f32[160,512]{1,0:T(8,128)S(1)} %get-tuple-element.76), channel_id=1, source_target_pairs={{0,2},{1,3},{2,0},{3,1},{4,6},{5,7},{6,4},{7,5},{8,10},{9,11},{10,... | collective-permute-start | bytes 983048 | tf_op jit(solution)/shard_map/ppermute | solution.py:274
  161.6 9.8 %collective-permute-start.14 = (f32[160,512]{1,0:T(8,128)S(1)}, f32[160,512]{1,0:T(8,128)S(1)}, u32[]{:S(2)}, u32[]{:S(2)}) collective-permute-start(f32[160,512]{1,0:T(8,128)S(1)} %get-tuple-element.77), channel_id=1, source_target_pairs={{0,1},{1,0},{2,3},{3,2},{4,5},{5,4},{6,7},{7,6},{8,9},{9,8},{10,11... | collective-permute-start | bytes 983048 | tf_op jit(solution)/shard_map/ppermute | solution.py:274
  223.8 176.7 %reduce-scatter.6.cloned.1.call-start = ((), (), s32[]{:S(2)}) async-start(), calls=%async_computation.10 | async-start | bytes 10485760 | tf_op jit(solution)/shard_map/reduce_scatter | solution.py:349
  247.4 289.0 %reduce-scatter.4.cloned.1.call-start = ((), (), s32[]{:S(2)}) async-start(), calls=%async_computation.9 | async-start | bytes 10485760 | tf_op jit(solution)/shard_map/reduce_scatter | solution.py:349
  320.0 8.2 %collective-permute-start.29 = (f32[160,512]{1,0:T(8,128)S(1)}, f32[160,512]{1,0:T(8,128)S(1)}, u32[]{:S(2)}, u32[]{:S(2)}) collective-permute-start(f32[160,512]{1,0:T(8,128)S(1)} %get-tuple-element.74), channel_id=1, source_target_pairs={{0,1},{1,0},{2,3},{3,2},{4,5},{5,4},{6,7},{7,6},{8,9},{9,8},{10,11... | collective-permute-start | bytes 983048 | tf_op jit(solution)/shard_map/ppermute | solution.py:274
  321.3 10.5 %collective-permute-start.31 = (f32[160,512]{1,0:T(8,128)S(1)}, f32[160,512]{1,0:T(8,128)S(1)}, u32[]{:S(2)}, u32[]{:S(2)}) collective-permute-start(f32[160,512]{1,0:T(8,128)S(1)} %get-tuple-element.75), channel_id=1, source_target_pairs={{0,2},{1,3},{2,0},{3,1},{4,6},{5,7},{6,4},{7,5},{8,10},{9,11},{10,... | collective-permute-start | bytes 983048 | tf_op jit(solution)/shard_map/ppermute | solution.py:274
  331.9 7.1 %collective-permute-start.30 = (f32[160,512]{1,0:T(8,128)S(1)}, f32[160,512]{1,0:T(8,128)S(1)}, u32[]{:S(2)}, u32[]{:S(2)}) collective-permute-start(f32[160,512]{1,0:T(8,128)S(1)} %get-tuple-element.72), channel_id=1, source_target_pairs={{0,2},{1,3},{2,0},{3,1},{4,6},{5,7},{6,4},{7,5},{8,10},{9,11},{10,... | collective-permute-start | bytes 983048 | tf_op jit(solution)/shard_map/ppermute | solution.py:274
  361.0 54.8 %all-to-all-start.2 = ((f32[8,64,1024]{2,1,0:T(8,128)}), f32[8,64,1024]{2,1,0:T(8,128)}, u32[]{:S(2)}, u32[]{:S(2)}) async-start(f32[8,64,1024]{2,1,0:T(8,128)} %bitcast.252), calls=%async_computation.5 | async-start | bytes 4194304 | tf_op jit(solution)/shard_map/all_to_all | solution.py:351
  376.5 60.0 %collective-permute-start.15 = (bf16[2,2,128,1024]{3,2,1,0:T(8,128)(2,1)}, bf16[2,2,128,1024]{3,2,1,0:T(8,128)(2,1)}, u32[]{:S(2)}, u32[]{:S(2)}) collective-permute-start(bf16[2,2,128,1024]{3,2,1,0:T(8,128)(2,1)} %pad_maximum_fusion.4), channel_id=1, source_target_pairs={{0,1},{1,0},{2,3},{3,2},{4,5},{5,4},{6,7},{7,6},{8,9},{9,8},{10,11... | collective-permute-start | bytes 3145736 | tf_op jit(solution)/shard_map/ppermute | solution.py:274
  380.0 139.1 %collective-permute-start.17 = (bf16[2,2,128,1024]{3,2,1,0:T(8,128)(2,1)}, bf16[2,2,128,1024]{3,2,1,0:T(8,128)(2,1)}, u32[]{:S(2)}, u32[]{:S(2)}) collective-permute-start(bf16[2,2,128,1024]{3,2,1,0:T(8,128)(2,1)} %pad_maximum_fusion.5), channel_id=1, source_target_pairs={{0,2},{1,3},{2,0},{3,1},{4,6},{5,7},{6,4},{7,5},{8,10},{9,11},{10,... | collective-permute-start | bytes 3145736 | tf_op jit(solution)/shard_map/ppermute | solution.py:274
  387.6 136.1 %collective-permute-start.38 = (f32[311,512]{1,0:T(8,128)}, f32[311,512]{1,0:T(8,128)}, u32[]{:S(2)}, u32[]{:S(2)}) collective-permute-start(f32[311,512]{1,0:T(8,128)} %constant_dynamic-slice_fusion), channel_id=1, source_target_pairs={{0,4},{1,5},{2,6},{3,7},{4,0},{5,1},{6,2},{7,3},{8,12},{9,13},{10,... | collective-permute-start | bytes 1910792 | tf_op jit(solution)/shard_map/ppermute | solution.py:274
  415.8 123.4 %all-to-all-start.1 = ((f32[8,64,1024]{2,1,0:T(8,128)}), f32[8,64,1024]{2,1,0:T(8,128)}, u32[]{:S(2)}, u32[]{:S(2)}) async-start(f32[8,64,1024]{2,1,0:T(8,128)} %bitcast.61), calls=%async_computation.3 | async-start | bytes 4194304 | tf_op jit(solution)/shard_map/all_to_all | solution.py:351
  420.2 142.3 %all-reduce.4.cloned.1.call-start = ((), (), s32[]{:S(2)}) async-start(), calls=%async_computation.11 | async-start | bytes 1277952 | tf_op jit(solution)/shard_map/psum | solution.py:466
  431.9 95.6 %collective-permute-start.33 = (bf16[2,2,128,1024]{3,2,1,0:T(8,128)(2,1)}, bf16[2,2,128,1024]{3,2,1,0:T(8,128)(2,1)S(1)}, u32[]{:S(2)}, u32[]{:S(2)}) collective-permute-start(bf16[2,2,128,1024]{3,2,1,0:T(8,128)(2,1)} %pad_maximum_fusion.6), channel_id=1, source_target_pairs={{0,1},{1,0},{2,3},{3,2},{4,5},{5,4},{6,7},{7,6},{8,9},{9,8},{10,11... | collective-permute-start | bytes 3145736 | tf_op jit(solution)/shard_map/ppermute | solution.py:274
  435.0 96.6 %collective-permute-start.35 = (bf16[2,2,128,1024]{3,2,1,0:T(8,128)(2,1)}, bf16[2,2,128,1024]{3,2,1,0:T(8,128)(2,1)S(1)}, u32[]{:S(2)}, u32[]{:S(2)}) collective-permute-start(bf16[2,2,128,1024]{3,2,1,0:T(8,128)(2,1)} %pad_maximum_fusion.7), channel_id=1, source_target_pairs={{0,2},{1,3},{2,0},{3,1},{4,6},{5,7},{6,4},{7,5},{8,10},{9,11},{10,... | collective-permute-start | bytes 3145736 | tf_op jit(solution)/shard_map/ppermute | solution.py:274
  438.7 87.0 %collective-permute-start.16 = (bf16[1,2,128,1024]{3,2,1,0:T(8,128)(2,1)}, bf16[1,2,128,1024]{3,2,1,0:T(8,128)(2,1)}, u32[]{:S(2)}, u32[]{:S(2)}) collective-permute-start(bf16[1,2,128,1024]{3,2,1,0:T(8,128)(2,1)} %fusion.35), channel_id=1, source_target_pairs={{0,2},{1,3},{2,0},{3,1},{4,6},{5,7},{6,4},{7,5},{8,10},{9,11},{10,... | collective-permute-start | bytes 1572872 | tf_op jit(solution)/shard_map/ppermute | solution.py:274
  521.4 13.2 %collective-permute-start.18 = (bf16[1,2,128,1024]{3,2,1,0:T(8,128)(2,1)}, bf16[1,2,128,1024]{3,2,1,0:T(8,128)(2,1)}, u32[]{:S(2)}, u32[]{:S(2)}) collective-permute-start(bf16[1,2,128,1024]{3,2,1,0:T(8,128)(2,1)} %fusion.33), channel_id=1, source_target_pairs={{0,1},{1,0},{2,3},{3,2},{4,5},{5,4},{6,7},{7,6},{8,9},{9,8},{10,11... | collective-permute-start | bytes 1572872 | tf_op jit(solution)/shard_map/ppermute | solution.py:274
  530.1 19.5 %collective-permute-start.34 = (bf16[1,2,128,1024]{3,2,1,0:T(8,128)(2,1)}, bf16[1,2,128,1024]{3,2,1,0:T(8,128)(2,1)}, u32[]{:S(2)}, u32[]{:S(2)}) collective-permute-start(bf16[1,2,128,1024]{3,2,1,0:T(8,128)(2,1)} %fusion.31), channel_id=1, source_target_pairs={{0,2},{1,3},{2,0},{3,1},{4,6},{5,7},{6,4},{7,5},{8,10},{9,11},{10,... | collective-permute-start | bytes 1572872 | tf_op jit(solution)/shard_map/ppermute | solution.py:274
  534.2 21.0 %collective-permute-start.36 = (bf16[1,2,128,1024]{3,2,1,0:T(8,128)(2,1)}, bf16[1,2,128,1024]{3,2,1,0:T(8,128)(2,1)}, u32[]{:S(2)}, u32[]{:S(2)}) collective-permute-start(bf16[1,2,128,1024]{3,2,1,0:T(8,128)(2,1)} %fusion.29), channel_id=1, source_target_pairs={{0,1},{1,0},{2,3},{3,2},{4,5},{5,4},{6,7},{7,6},{8,9},{9,8},{10,11... | collective-permute-start | bytes 1572872 | tf_op jit(solution)/shard_map/ppermute | solution.py:274
  539.3 109.3 %all-to-all-start = ((f32[8,64,1024]{2,1,0:T(8,128)}), f32[8,64,1024]{2,1,0:T(8,128)}, u32[]{:S(2)}, u32[]{:S(2)}) async-start(f32[8,64,1024]{2,1,0:T(8,128)} %bitcast.248), calls=%async_computation.1 | async-start | bytes 4194304 | tf_op jit(solution)/shard_map/all_to_all | solution.py:351
  546.6 81.6 %collective-permute-start.19 = (bf16[128,2048]{1,0:T(8,128)(2,1)}, bf16[128,2048]{1,0:T(8,128)(2,1)}, u32[]{:S(2)}, u32[]{:S(2)}) collective-permute-start(bf16[128,2048]{1,0:T(8,128)(2,1)} %fusion.47), channel_id=1, source_target_pairs={{0,4},{1,5},{2,6},{3,7},{4,0},{5,1},{6,2},{7,3},{8,12},{9,13},{10,... | collective-permute-start | bytes 1572872 | tf_op jit(solution)/shard_map/ppermute | solution.py:274
  558.6 77.0 %collective-permute-start.37 = (bf16[128,2048]{1,0:T(8,128)(2,1)}, bf16[128,2048]{1,0:T(8,128)(2,1)}, u32[]{:S(2)}, u32[]{:S(2)}) collective-permute-start(bf16[128,2048]{1,0:T(8,128)(2,1)} %fusion.48), channel_id=1, source_target_pairs={{0,4},{1,5},{2,6},{3,7},{4,0},{5,1},{6,2},{7,3},{8,12},{9,13},{10,... | collective-permute-start | bytes 1572872 | tf_op jit(solution)/shard_map/ppermute | solution.py:274
  (59 other events, 941.6 us)
Sparse Core Ops, SparseCore 0:
  10.6 37.1 all-gather.3
  49.9 34.4 all-gather.5
  86.6 34.4 all-gather.7
  223.9 71.5 reduce-scatter.7
  298.1 71.7 reduce-scatter.5
  372.3 71.7 reduce-scatter.3
  525.9 32.7 all-reduce.3

commit v2 on v1

v2 whole, which is shorter than its diff:
```python
from functools import partial

import jax
import jax.numpy as jnp
from jax import lax
from jax.experimental import pallas as pl
from jax.experimental.pallas import tpu as pltpu
from jax.sharding import Mesh
from jax.sharding import PartitionSpec as P

EPS = 1e-05
LOG2E = 1.4426950408889634
NT = (((1,), (1,)), ((), ()))
TN = (((0,), (0,)), ((), ()))
ROWS = 128
LANES = 256
SUB = 16


def gate(values, *earlier):
    count = len(values)
    anywhere = pl.BlockSpec(memory_space=pl.ANY)
    return pl.pallas_call(
        lambda *refs: None,
        in_specs=[anywhere] * (count + len(earlier)),
        out_specs=[anywhere] * count,
        out_shape=[jax.ShapeDtypeStruct(value.shape, value.dtype) for value in values],
        input_output_aliases={at: at for at in range(count)},
        name="gate",
    )(*values, *earlier)


def softplus(x):
    e = jnp.exp(-jnp.abs(x))
    return jnp.maximum(x, 0.0) + jnp.log1p(e)


def block_diagonal(columns, states):
    wide = SUB * states
    lane = lax.broadcasted_iota(jnp.int32, (states, wide), 1)
    row = lax.broadcasted_iota(jnp.int32, (states, wide), 0)
    tile = (lax.rem(lane, states) == row).astype(jnp.bfloat16)
    spread = lax.dot_general(columns.astype(jnp.bfloat16), tile, TN, preferred_element_type=jnp.float32)
    block = lax.broadcasted_iota(jnp.int32, (ROWS, wide), 1) // states
    step = lax.rem(lax.broadcasted_iota(jnp.int32, (ROWS, wide), 0), SUB)
    return jnp.where(block == step, spread, 0.0).astype(jnp.bfloat16)


def scan_forward_kernel(
    low_rank, states, lanes,
    order_ref, sel_ref, u_ref, dtp_ref, bias_ref, alog_ref, skip_ref, start_ref,
    *refs,
):
    y_ref, h_ref, delta_ref, sig_ref, end_ref, state, pre, weighted, diag, decay = refs[-10:]
    chan = u_ref.shape[1]

    @pl.when(pl.program_id(0) == 0)
    def _():
        state[...] = start_ref[...]
        decay[...] = -jnp.exp(alog_ref[...]) * LOG2E

    low = sel_ref[:low_rank, :].astype(jnp.bfloat16)
    pre[...] = lax.dot_general(low, dtp_ref[...], TN, preferred_element_type=jnp.float32)
    entry = sel_ref[low_rank : low_rank + states, :]
    diag[...] = block_diagonal(sel_ref[low_rank + states :, :], states)

    def piece(sub, _):
        base = pl.multiple_of(sub * SUB, SUB)
        rows = pl.ds(base, SUB)
        size = pre[rows, :] + bias_ref[...]
        delta = softplus(size)
        delta_ref[rows, :] = delta
        sig_ref[rows, :] = jnp.exp(size - delta).astype(jnp.bfloat16)
        u_float = u_ref[rows, :].astype(jnp.float32)
        weighted[rows, :] = delta * u_float
        cols = pltpu.roll(entry, lax.rem(ROWS - base, ROWS), 1)
        for start in range(0, chan, lanes):
            at = pl.ds(start, lanes)
            rate = decay[:, at]
            hidden = state[:, at]
            for step in range(SUB):
                row = pl.ds(base + step, 1)
                grow = jnp.exp2(delta_ref[row, at] * rate)
                hidden = grow * hidden + cols[:, step : step + 1] * weighted[row, at]
                h_ref[pl.ds(pl.multiple_of((base + step) * states, states), states), at] = hidden.astype(jnp.bfloat16)
            state[:, at] = hidden
            held = h_ref[pl.ds(pl.multiple_of(base * states, SUB * states), SUB * states), at]
            out = jnp.dot(diag[rows, :], held, preferred_element_type=jnp.float32)
            y_ref[rows, at] = (out + skip_ref[:, at] * u_float[:, start : start + lanes]).astype(jnp.bfloat16)
        return 0

    lax.fori_loop(0, ROWS // SUB, piece, 0)
    end_ref[...] = state[...]


def scan_forward(order, first, count, select, u_act, dt_proj, dt_bias, a_log, d_skip, start, held=(), needs=()):
    length, chan = u_act.shape
    states = a_log.shape[0]
    low_rank = dt_proj.shape[0]
    lanes = min(LANES, chan)
    whole = lambda shape: pl.BlockSpec(shape, lambda i, order: (0, 0))
    by_rows = pl.BlockSpec((ROWS, chan), lambda i, order: (order[first + i], 0))
    in_time = pl.BlockSpec((ROWS, chan), lambda i, order: (i, 0))
    spec = pltpu.PrefetchScalarGridSpec(
        num_scalar_prefetch=1,
        grid=(count,),
        in_specs=[
            pl.BlockSpec((select.shape[0], ROWS), lambda i, order: (0, first + i)),
            by_rows,
            whole((low_rank, chan)),
            whole((1, chan)),
            whole((states, chan)),
            whole((1, chan)),
            whole((states, chan)),
        ]
        + [pl.BlockSpec(memory_space=pl.ANY)] * (len(held) + len(needs)),
        out_specs=[
            by_rows,
            pl.BlockSpec((ROWS * states, chan), lambda i, order: (i, 0)),
            in_time,
            in_time,
            whole((states, chan)),
        ],
        scratch_shapes=[
            pltpu.VMEM((states, chan), jnp.float32),
            pltpu.VMEM((ROWS, chan), jnp.float32),
            pltpu.VMEM((ROWS, chan), jnp.float32),
            pltpu.VMEM((ROWS, SUB * states), jnp.bfloat16),
            pltpu.VMEM((states, chan), jnp.float32),
        ],
    )
    rows = count * ROWS
    return pl.pallas_call(
        partial(scan_forward_kernel, low_rank, states, lanes),
        grid_spec=spec,
        out_shape=[
            jax.ShapeDtypeStruct((length, chan), jnp.bfloat16),
            jax.ShapeDtypeStruct((rows * states, chan), jnp.bfloat16),
            jax.ShapeDtypeStruct((rows, chan), jnp.float32),
            jax.ShapeDtypeStruct((rows, chan), jnp.bfloat16),
            jax.ShapeDtypeStruct((states, chan), jnp.float32),
        ],
        input_output_aliases={8 + at: at for at in range(len(held))},
        compiler_params=pltpu.CompilerParams(vmem_limit_bytes=40 * 2**20),
        cost_estimate=pl.CostEstimate(
            flops=12 * rows * states * chan,
            bytes_accessed=140 * rows * chan,
            transcendentals=rows * states * chan,
        ),
        name="scan_forward",
    )(order, select, u_act, dt_proj, dt_bias.reshape(1, chan), a_log, d_skip.reshape(1, chan), start, *held, *needs)


def scan_backward_kernel(
    low_rank, states, lanes,
    order_ref, sel_ref, h_ref, before_ref, start_ref, delta_ref, sig_ref, u_ref, dy_ref, dtp_ref, alog_ref, skip_ref,
    passed_ref, dec_in, bias_in, skip_in, proj_in,
    *refs,
):
    upart_ref, part_ref, dec_ref, bias_ref, skipg_ref, proj_ref, left_ref = refs[-19:-12]
    carry, dyf, weighted, diag, decay, rates16, gbuf, abuf, dbuf, ents, rdos, pre_ref = refs[-12:]
    chan = u_ref.shape[1]
    wide = SUB * states
    step_id = pl.program_id(0)
    last = pl.num_programs(0) - 1

    @pl.when(step_id == 0)
    def _():
        carry[...] = passed_ref[...]
        rates = -jnp.exp(alog_ref[...])
        decay[...] = rates * LOG2E
        rates16[...] = rates.astype(jnp.bfloat16)
        dec_ref[...] = dec_in[...]
        bias_ref[...] = bias_in[...]
        skipg_ref[...] = skip_in[...]
        proj_ref[...] = proj_in[...]

    readout = sel_ref[low_rank + states :, :]
    diag[...] = block_diagonal(sel_ref[low_rank : low_rank + states, :], states)
    block = lax.broadcasted_iota(jnp.int32, (SUB, wide), 1) // states
    inside = block == lax.broadcasted_iota(jnp.int32, (SUB, wide), 0)
    ones = jnp.where(inside, 1.0, 0.0).astype(jnp.bfloat16)
    member = lax.rem(lax.broadcasted_iota(jnp.int32, (states, wide), 1), states)
    gather = jnp.where(member == lax.broadcasted_iota(jnp.int32, (states, wide), 0), 1.0, 0.0).astype(jnp.bfloat16)

    def piece(index, _):
        sub = ROWS // SUB - 1 - index
        base = pl.multiple_of(sub * SUB, SUB)
        rows = pl.ds(base, SUB)
        hrows = pl.ds(pl.multiple_of(base * states, wide), wide)
        u_float = u_ref[rows, :].astype(jnp.float32)
        delta = delta_ref[rows, :]
        dy_float = dy_ref[rows, :].astype(jnp.float32)
        dyf[...] = dy_float
        weighted[...] = (delta * u_float).astype(jnp.bfloat16)
        cols = pltpu.roll(readout, lax.rem(ROWS - base, ROWS), 1)
        first = lax.max(base * states - states, 0)
        ent = jnp.zeros((SUB, wide), jnp.float32)
        rdo = jnp.zeros((SUB, wide), jnp.float32)
        for start in range(0, chan, lanes):
            at = pl.ds(start, lanes)
            rate = decay[:, at]
            rate16 = rates16[:, at]
            passed = carry[:, at]
            inner = h_ref[pl.ds(pl.multiple_of(first, states), states), at]
            outer = jnp.where(step_id == last, start_ref[:, at].astype(jnp.bfloat16), before_ref[:, at])
            earliest = jnp.where(sub == 0, outer, inner)
            for step in reversed(range(SUB)):
                row = pl.ds(base + step, 1)
                size = jnp.broadcast_to(delta_ref[row, at], (states, lanes))
                grow = jnp.exp2(size * rate)
                grad = cols[:, step : step + 1] * dyf[pl.ds(step, 1), at] + passed
                passed = grow * grad
                if step:
                    earlier = h_ref[pl.ds(pl.multiple_of((base + step - 1) * states, states), states), at]
                else:
                    earlier = earliest
                logg = passed.astype(jnp.bfloat16) * earlier
                here = pl.ds(step * states, states)
                gbuf[here, at] = grad.astype(jnp.bfloat16)
                abuf[here, at] = logg * rate16
                dbuf[here, at] = logg * size.astype(jnp.bfloat16)
            carry[:, at] = passed
            shared = jnp.dot(diag[rows, :], gbuf[:, at], preferred_element_type=jnp.float32)
            size_a = jnp.dot(ones, abuf[:, at], preferred_element_type=jnp.float32)
            dec_ref[:, at] += jnp.dot(gather, dbuf[:, at], preferred_element_type=jnp.float32)
            rdo += lax.dot_general(dy_ref[rows, at], h_ref[hrows, at], NT, preferred_element_type=jnp.float32)
            ent += lax.dot_general(weighted[:, at], gbuf[:, at], NT, preferred_element_type=jnp.float32)
            u_here = u_float[:, start : start + lanes]
            dy_here = dy_float[:, start : start + lanes]
            pre16 = ((size_a + shared * u_here) * sig_ref[rows, at].astype(jnp.float32)).astype(jnp.bfloat16)
            pre_ref[rows, at] = pre16
            bias_ref[:, at] += jnp.sum(pre16.astype(jnp.float32), axis=0, keepdims=True)
            skipg_ref[:, at] += jnp.sum(dy_here * u_here, axis=0, keepdims=True)
            upart_ref[rows, at] = shared * delta[:, start : start + lanes] + skip_ref[:, at] * dy_here
        ents[rows, :] = jnp.where(inside, ent, 0.0)
        rdos[rows, :] = jnp.where(inside, rdo, 0.0)
        return 0

    lax.fori_loop(0, ROWS // SUB, piece, 0)
    part_ref[:low_rank, :] = lax.dot_general(dtp_ref[...], pre_ref[...], NT, preferred_element_type=jnp.float32)
    low = sel_ref[:low_rank, :].astype(jnp.bfloat16)
    proj_ref[...] += jnp.dot(low, pre_ref[...], preferred_element_type=jnp.float32)
    whole = gather.astype(jnp.float32)
    for at, rows in ((low_rank, ents), (low_rank + states, rdos)):
        part_ref[at : at + states, :] = lax.dot_general(
            whole, rows[...], NT, precision=lax.Precision.HIGHEST, preferred_element_type=jnp.float32
        )
    left_ref[...] = carry[...]


def scan_backward(
    order, first, count, select, hidden, start, delta, sig, u_act, y_grad, dt_proj, a_log, d_skip, passed, sums, held=(), needs=()
):
    length, chan = u_act.shape
    states = a_log.shape[0]
    low_rank = dt_proj.shape[0]
    lanes = min(LANES, chan)
    wide = SUB * states
    rows = count * ROWS
    here = lambda i: count - 1 - i
    whole = lambda shape: pl.BlockSpec(shape, lambda i, order: (0, 0))
    by_rows = pl.BlockSpec((ROWS, chan), lambda i, order: (order[first + here(i)], 0))
    in_time = pl.BlockSpec((ROWS, chan), lambda i, order: (here(i), 0))
    by_cols = pl.BlockSpec((select.shape[0], ROWS), lambda i, order: (0, first + here(i)))
    before = pl.BlockSpec((states, chan), lambda i, order: (lax.max(here(i) - 1, 0) * ROWS + ROWS - 1, 0))
    spec = pltpu.PrefetchScalarGridSpec(
        num_scalar_prefetch=1,
        grid=(count,),
        in_specs=[
            by_cols,
            pl.BlockSpec((ROWS * states, chan), lambda i, order: (here(i), 0)),
            before,
            whole((states, chan)),
            in_time,
            in_time,
            by_rows,
            by_rows,
            whole((low_rank, chan)),
            whole((states, chan)),
            whole((1, chan)),
            whole((states, chan)),
            whole((states, chan)),
            whole((1, chan)),
            whole((1, chan)),
            whole((low_rank, chan)),
        ]
        + [pl.BlockSpec(memory_space=pl.ANY)] * (len(held) + len(needs)),
        out_specs=[
            pl.BlockSpec((ROWS, chan), lambda i, order: (first + here(i), 0)),
            by_cols,
            whole((states, chan)),
            whole((1, chan)),
            whole((1, chan)),
            whole((low_rank, chan)),
            whole((states, chan)),
        ],
        scratch_shapes=[
            pltpu.VMEM((states, chan), jnp.float32),
            pltpu.VMEM((SUB, chan), jnp.float32),
            pltpu.VMEM((SUB, chan), jnp.bfloat16),
            pltpu.VMEM((ROWS, wide), jnp.bfloat16),
            pltpu.VMEM((states, chan), jnp.float32),
            pltpu.VMEM((states, chan), jnp.bfloat16),
            pltpu.VMEM((wide, chan), jnp.bfloat16),
            pltpu.VMEM((wide, chan), jnp.bfloat16),
            pltpu.VMEM((wide, chan), jnp.bfloat16),
            pltpu.VMEM((ROWS, wide), jnp.float32),
            pltpu.VMEM((ROWS, wide), jnp.float32),
            pltpu.VMEM((ROWS, chan), jnp.bfloat16),
        ],
    )
    return pl.pallas_call(
        partial(scan_backward_kernel, low_rank, states, lanes),
        grid_spec=spec,
        out_shape=[
            jax.ShapeDtypeStruct((length, chan), jnp.float32),
            jax.ShapeDtypeStruct(select.shape, jnp.float32),
            jax.ShapeDtypeStruct((states, chan), jnp.float32),
            jax.ShapeDtypeStruct((1, chan), jnp.float32),
            jax.ShapeDtypeStruct((1, chan), jnp.float32),
            jax.ShapeDtypeStruct((low_rank, chan), jnp.float32),
            jax.ShapeDtypeStruct((states, chan), jnp.float32),
        ],
        input_output_aliases={17 + at: at for at in range(len(held))},
        compiler_params=pltpu.CompilerParams(vmem_limit_bytes=40 * 2**20),
        cost_estimate=pl.CostEstimate(
            flops=30 * rows * states * chan,
            bytes_accessed=220 * rows * chan,
            transcendentals=rows * states * chan,
        ),
        name="scan_backward",
    )(
        order, select, hidden, hidden, start, delta, sig, u_act, y_grad, dt_proj, a_log, d_skip.reshape(1, chan),
        passed, *sums, *held, *needs,
    )


def taps_of(window, rows, count):
    return [window[8 - (count - 1) + tap : 8 - (count - 1) + tap + rows, :] for tap in range(count)]


def conv_forward_kernel(lanes, order_ref, x_ref, w_ref, b_ref, proj_ref, *refs):
    u_ref, part_ref, tail = refs[-3:]
    rows, chan = x_ref.shape
    taps = w_ref.shape[0]

    @pl.when(pl.program_id(0) == 0)
    def _():
        tail[...] = jnp.zeros_like(tail)

    total = jnp.zeros(part_ref.shape, jnp.float32)
    for start in range(0, chan, lanes):
        at = pl.ds(start, lanes)
        values = x_ref[:, at].astype(jnp.float32)
        window = jnp.concatenate([tail[:, at], values], axis=0)
        tail[:, at] = values[rows - 8 :, :]
        pre = b_ref[:, at] + sum(w_ref[tap : tap + 1, at] * part for tap, part in enumerate(taps_of(window, rows, taps)))
        act = (pre / (1.0 + jnp.exp(-pre))).astype(jnp.bfloat16)
        u_ref[:, at] = act
        total = total + lax.dot_general(proj_ref[:, at], act, NT, preferred_element_type=jnp.float32)
    part_ref[...] = total


def conv_forward(order, x_part, conv_w, conv_b, sel_proj, needs=()):
    length, chan = x_part.shape
    wide = sel_proj.shape[0]
    whole = lambda shape: pl.BlockSpec(shape, lambda i, order: (0, 0))
    by_rows = pl.BlockSpec((ROWS, chan), lambda i, order: (order[i], 0))
    spec = pltpu.PrefetchScalarGridSpec(
        num_scalar_prefetch=1,
        grid=(length // ROWS,),
        in_specs=[by_rows, whole(conv_w.shape), whole((1, chan)), whole((wide, chan))]
        + [pl.BlockSpec(memory_space=pl.ANY)] * len(needs),
        out_specs=[by_rows, pl.BlockSpec((wide, ROWS), lambda i, order: (0, i))],
        scratch_shapes=[pltpu.VMEM((8, chan), jnp.float32)],
    )
    return pl.pallas_call(
        partial(conv_forward_kernel, min(256, chan)),
        grid_spec=spec,
        out_shape=[
            jax.ShapeDtypeStruct((length, chan), jnp.bfloat16),
            jax.ShapeDtypeStruct((wide, length), jnp.float32),
        ],
        compiler_params=pltpu.CompilerParams(vmem_limit_bytes=40 * 2**20),
        cost_estimate=pl.CostEstimate(
            flops=2 * wide * length * chan, bytes_accessed=22 * length * chan, transcendentals=length * chan
        ),
        name="conv_forward",
    )(order, x_part, conv_w, conv_b, sel_proj, *needs)


def conv_backward_kernel(
    lanes,
    order_ref, x_ref, before_ref, upart_ref, sgrad_ref, w_ref, b_ref, proj_ref, alog_ref,
    dec_ref, dbias_ref, dskip_ref, dproj_ref,
    *refs,
):
    xgrad_ref, stack_ref, head, wgrad, bgrad, pgrad = refs[-6:]
    rows, chan = x_ref.shape
    taps = w_ref.shape[0]
    last = pl.num_programs(0) - 1
    first = pl.program_id(0) == last

    @pl.when(pl.program_id(0) == 0)
    def _():
        head[...] = jnp.zeros_like(head)
        wgrad[...] = jnp.zeros_like(wgrad)
        bgrad[...] = jnp.zeros_like(bgrad)
        pgrad[...] = jnp.zeros_like(pgrad)

    sgrad = sgrad_ref[...].astype(jnp.bfloat16)
    for start in range(0, chan, lanes):
        at = pl.ds(start, lanes)
        earlier = before_ref[8:, at].astype(jnp.float32)
        window = jnp.concatenate([jnp.where(first, 0.0, earlier), x_ref[:, at].astype(jnp.float32)], axis=0)
        parts = taps_of(window, rows, taps)
        pre = b_ref[:, at] + sum(w_ref[tap : tap + 1, at] * part for tap, part in enumerate(parts))
        sig = 1.0 / (1.0 + jnp.exp(-pre))
        act = (pre * sig).astype(jnp.bfloat16)
        u_grad = upart_ref[:, at] + lax.dot_general(sgrad, proj_ref[:, at], TN, preferred_element_type=jnp.float32)
        grad = u_grad * (sig * (1.0 + pre * (1.0 - sig)))
        bgrad[:, at] += jnp.sum(grad, axis=0, keepdims=True)
        wgrad[:, at] += jnp.concatenate([jnp.sum(grad * part, axis=0, keepdims=True) for part in parts], axis=0)
        pgrad[:, at] += jnp.dot(sgrad, act, preferred_element_type=jnp.float32)
        later = jnp.concatenate([grad, head[:, at]], axis=0)
        head[:, at] = grad[:8, :]
        x_grad = sum(w_ref[tap : tap + 1, at] * later[taps - 1 - tap : taps - 1 - tap + rows, :] for tap in range(taps))
        xgrad_ref[:, at] = x_grad.astype(jnp.bfloat16)

    @pl.when(pl.program_id(0) == last)
    def _():
        half = chan // 2
        stack_ref[...] = jnp.zeros_like(stack_ref)
        terms = (pgrad[...], dproj_ref[...], dec_ref[...] * -jnp.exp(alog_ref[...]), wgrad[...], bgrad[...],
                 dbias_ref[...], dskip_ref[...])
        at = 0
        for term in terms:
            for side in range(2):
                stack_ref[side, at : at + term.shape[0], :] = term[:, side * half : (side + 1) * half]
            at += term.shape[0]


def conv_backward(order, x_part, u_part, select_grad, conv_w, conv_b, sel_proj, a_log, sums, needs=()):
    length, chan = x_part.shape
    wide = sel_proj.shape[0]
    count = length // ROWS
    high = -(-(wide + conv_w.shape[0] + 1 + sum(term.shape[0] for term in sums)) // 16) * 16
    whole = lambda shape: pl.BlockSpec(shape, lambda i, order: (0, 0))
    at = lambda i, order: order[count - 1 - i]
    by_rows = pl.BlockSpec((ROWS, chan), lambda i, order: (at(i, order), 0))
    before = pl.BlockSpec((16, chan), lambda i, order: ((order[lax.max(count - 2 - i, 0)] + 1) * (ROWS // 16) - 1, 0))
    spec = pltpu.PrefetchScalarGridSpec(
        num_scalar_prefetch=1,
        grid=(count,),
        in_specs=[
            by_rows,
            before,
            pl.BlockSpec((ROWS, chan), lambda i, order: (count - 1 - i, 0)),
            pl.BlockSpec((wide, ROWS), lambda i, order: (0, count - 1 - i)),
            whole(conv_w.shape),
            whole((1, chan)),
            whole((wide, chan)),
            whole(a_log.shape),
        ]
        + [whole(term.shape) for term in sums]
        + [pl.BlockSpec(memory_space=pl.ANY)] * len(needs),
        out_specs=[by_rows, pl.BlockSpec((2, high, chan // 2), lambda i, order: (0, 0, 0))],
        scratch_shapes=[
            pltpu.VMEM((8, chan), jnp.float32),
            pltpu.VMEM(conv_w.shape, jnp.float32),
            pltpu.VMEM((1, chan), jnp.float32),
            pltpu.VMEM((wide, chan), jnp.float32),
        ],
    )
    return pl.pallas_call(
        partial(conv_backward_kernel, min(256, chan)),
        grid_spec=spec,
        out_shape=[
            jax.ShapeDtypeStruct((length, chan), jnp.bfloat16),
            jax.ShapeDtypeStruct((2, high, chan // 2), jnp.float32),
        ],
        compiler_params=pltpu.CompilerParams(vmem_limit_bytes=40 * 2**20),
        cost_estimate=pl.CostEstimate(
            flops=4 * wide * length * chan, bytes_accessed=40 * length * chan, transcendentals=length * chan
        ),
        name="conv_backward",
    )(order, x_part, x_part, u_part, select_grad, conv_w, conv_b, sel_proj, a_log, *sums, *needs)


def weight_rows_kernel(x_ref, others_ref, in_ref, out_ref):
    group = others_ref.shape[0]
    cols = x_ref.shape[3] // 2
    inner = out_ref.shape[1]
    for place in range(group):
        for turn in range(2):
            at = (turn * group + place) * cols
            here = slice(turn * cols, (turn + 1) * cols)
            total = x_ref[0, place, :, here].astype(jnp.float32) + x_ref[1, place, :, here].astype(jnp.float32)
            in_ref[:, at : at + cols] = total
            in_ref[:, inner + at : inner + at + cols] = others_ref[place, :, here].astype(jnp.float32)
            out_cols = slice((2 + turn) * cols, (3 + turn) * cols)
            out_ref[:, at : at + cols] = others_ref[place, :, out_cols].astype(jnp.float32)


def weight_rows(x_pieces, others):
    group, rows, wide = others.shape
    inner = group * wide // 2
    return pl.pallas_call(
        weight_rows_kernel,
        out_shape=[
            jax.ShapeDtypeStruct((rows, 2 * inner), jnp.float32),
            jax.ShapeDtypeStruct((rows, inner), jnp.float32),
        ],
        compiler_params=pltpu.CompilerParams(vmem_limit_bytes=40 * 2**20),
        name="weight_rows",
    )(x_pieces, others)


def interleave_kernel(near_ref, far_ref, both_ref):
    both_ref[0, 0] = near_ref[0]
    both_ref[0, 1] = far_ref[0]


def interleave(near, far):
    group, rows, width = near.shape
    block = pl.BlockSpec((1, rows, width), lambda i: (i, 0, 0))
    both = pl.pallas_call(
        interleave_kernel,
        grid=(group,),
        in_specs=[block, block],
        out_specs=pl.BlockSpec((1, 2, rows, width), lambda i: (i, 0, 0, 0)),
        out_shape=jax.ShapeDtypeStruct((group, 2, rows, width), near.dtype),
        name="interleave",
    )(near, far)
    return both.reshape(-1, width)


def silu_slope(values):
    sigmoid_value = jax.nn.sigmoid(values)
    return sigmoid_value * (1.0 + values * (1.0 - sigmoid_value))


def tie(index, *needs):
    for need in needs:
        first = need.reshape(-1)[:1].reshape(())
        index = index + (first != first).astype(jnp.int32)
    return index


def swap(values, axis, bit=1):
    return lax.ppermute(values, axis, [(index, index ^ bit) for index in range(lax.axis_size(axis))])


def sum_over_group(values, axis, sent=jnp.float32):
    size = lax.axis_size("quarter")
    bits = [1 << place for place in range(size.bit_length() - 1)]
    count = max(len(bits), 1)
    done = []
    for turn, part in enumerate(jnp.split(values, count, axis=axis)):
        for bit in bits[turn:] + bits[:turn]:
            part = part + swap(part.astype(sent), "quarter", bit).astype(jnp.float32)
        done.append(part)
    return jnp.concatenate(done, axis=axis)


def spread(blocks):
    copies = jnp.broadcast_to(blocks[None], (lax.axis_size("quarter"),) + blocks.shape)
    return lax.all_to_all(copies, "quarter", split_axis=0, concat_axis=0, tiled=True)


def collect(terms):
    terms = terms.reshape(lax.axis_size("quarter"), -1, terms.shape[-1])
    return lax.all_to_all(terms, "quarter", split_axis=0, concat_axis=0, tiled=True)


def sum_over(values, axis):
    size = lax.axis_size(axis)
    for place in range(size.bit_length() - 1):
        values = values + swap(values, axis, 1 << place)
    return values


def own_columns(weight, start, cols, place):
    group = lax.axis_size("quarter")
    return jnp.concatenate(
        [lax.dynamic_slice_in_dim(weight, start + (place + turn * group) * cols, cols, 1) for turn in range(2)], axis=1
    )


def both_blocks(values, half):
    other = swap(values, "half")
    return jnp.concatenate([jnp.where(half == 0, values, other), jnp.where(half == 0, other, values)], axis=-1)


def reduce_rows_by_swaps(terms):
    size, index = lax.axis_size("fsdp"), lax.axis_index("fsdp")
    terms = terms.reshape(size, -1, terms.shape[-1])
    for place in range(size.bit_length() - 1):
        bit = lax.rem(index >> place, 2)
        pairs = terms.reshape((-1, 2) + terms.shape[1:])
        kept, sent = [lax.dynamic_index_in_dim(pairs, which, 1, keepdims=False) for which in (bit, 1 - bit)]
        got = swap(sent.astype(jnp.bfloat16), "fsdp", 1 << place)
        terms = kept.astype(jnp.float32) + got.astype(jnp.float32)
    return terms[0]


def reduce_rows(terms, axis):
    return lax.psum_scatter(terms, axis, scatter_dimension=0, tiled=True)


def in_order(half, mine, other):
    return jnp.stack([jnp.where(half == 0, mine, other), jnp.where(half == 0, other, mine)])


def shards(
    hidden_in,
    cotangent,
    lengths,
    norm_gain,
    w_in,
    conv_w,
    conv_b,
    x_proj,
    dt_proj_w,
    dt_bias,
    a_log,
    d_skip,
    w_out,
):
    half, place = lax.axis_index("half"), lax.axis_index("quarter")
    group = lax.axis_size("quarter")
    rows_dev, width = hidden_in.shape[1:]
    length = 2 * group * rows_dev
    mid = length // 2
    cols = conv_b.shape[0]
    inner = w_out.shape[1]
    states, low_rank = a_log.shape[0], dt_proj_w.shape[0]
    taps = conv_w.shape[0]
    bf16, f32 = jnp.bfloat16, jnp.float32
    pick = lambda values, which: lax.dynamic_index_in_dim(values, which, 0, keepdims=False)

    flat = hidden_in.astype(f32)
    inverse = lax.rsqrt(jnp.mean(flat * flat, axis=-1, keepdims=True) + EPS)
    scaled = flat * inverse
    normed = (scaled * norm_gain).astype(bf16)
    crossed = swap(pick(normed, 1 - half), "half")
    near = spread(pick(normed, half))
    far = spread(gate([crossed], near)[0])

    later = lax.optimization_barrier((place, normed))[0]
    w_x = lax.all_gather(own_columns(w_in, 0, cols, later), "fsdp", axis=0, tiled=True)
    w_z = lax.all_gather(own_columns(w_in, inner, cols, later), "fsdp", axis=0, tiled=True)
    w_o = lax.all_gather(own_columns(w_out, 0, cols, later), "fsdp", axis=0, tiled=True)

    x_near, x_far = [
        jnp.dot(rows.reshape(mid, width), w_x, preferred_element_type=f32).astype(bf16) for rows in (near, far)
    ]
    x_part = jnp.stack([part.reshape(group, rows_dev, -1) for part in (x_near, x_far)], axis=1).reshape(length, -1)
    tokens = interleave(near, far)
    cot_other = pick(cotangent, tie(1 - half, far))

    blocks = lax.iota(jnp.int32, 2 * group)
    order = lax.rem(blocks, group) * 2 + (blocks // group != half).astype(jnp.int32)
    time_block = (lax.rem(blocks, 2) ^ half) * group + blocks // 2
    position = (time_block[:, None] * rows_dev + lax.iota(jnp.int32, rows_dev)[None]).reshape(length, 1)

    small = jnp.concatenate([conv_w, conv_b[None], dt_bias[None], a_log, d_skip[None]], axis=0)
    small = both_blocks(lax.optimization_barrier((small, crossed))[0], half)
    conv_taps, conv_bias, step_bias = small[:taps], small[taps : taps + 1], small[taps + 1]
    log_rates, skip = small[taps + 2 : taps + 2 + states], small[taps + 2 + states]
    proj = both_blocks(lax.optimization_barrier((jnp.concatenate([x_proj, dt_proj_w], axis=0), crossed))[0], half)
    sel_proj, size_proj = proj[: x_proj.shape[0]], proj[x_proj.shape[0] :]

    u_act, select_part = conv_forward(order, x_part, conv_taps, conv_bias, sel_proj)
    select = sum_over_group(select_part, 1)

    cot_near = spread(pick(cotangent, tie(half, select)))
    cot_crossed = swap(gate([cot_other], select)[0], "half")
    blank = jnp.zeros((states, 2 * cols), f32)
    y_sent, held, delta, sig, _ = scan_forward(
        order, 0, 2 * group, select, u_act, size_proj, step_bias, log_rates, skip, blank
    )
    cot_far = spread(gate([cot_crossed], y_sent)[0])
    w_z = gate([w_z], y_sent)[0]
    z_part = jnp.dot(tokens, w_z, preferred_element_type=f32)
    z_gate = jax.nn.silu(z_part)
    valid = (position < pick(lengths, half)).astype(f32)
    y_float = y_sent.astype(f32)
    gated = lax.optimization_barrier((valid * y_float * z_gate).astype(bf16))
    branch_terms = lax.dot_general(gated, w_o, NT, preferred_element_type=f32).astype(bf16)
    branch_got = collect(branch_terms)

    cot = interleave(gate([cot_near], y_sent)[0], gate([cot_far], z_part, branch_terms)[0])
    gated_grad = valid * jnp.dot(cot, w_o, preferred_element_type=f32)
    y_grad = (gated_grad * z_gate).astype(bf16)
    z_grad = (gated_grad * y_float * silu_slope(z_part)).astype(bf16)
    y_grad, z_grad = lax.optimization_barrier((y_grad, z_grad))
    out_term = lax.dot_general(cot, gated, TN, preferred_element_type=f32).astype(bf16)
    out_rows = reduce_rows(out_term, "fsdp")
    z_term = lax.dot_general(tokens, z_grad, TN, preferred_element_type=f32).astype(bf16)
    z_rows = reduce_rows(z_term, "fsdp")

    sums = (blank, jnp.zeros((1, 2 * cols), f32), jnp.zeros((1, 2 * cols), f32), jnp.zeros((low_rank, 2 * cols), f32))
    u_part, select_part, *sums, _ = scan_backward(
        order, 0, 2 * group, select, held, blank, delta, sig, u_act, y_grad, size_proj, log_rates, skip, blank, sums,
        needs=[out_term, z_term, branch_terms],
    )
    select_part = gate([select_part], branch_got)[0]
    z_normed = lax.dot_general(z_grad, w_z, NT, preferred_element_type=f32).astype(bf16)
    select_grad = sum_over_group(select_part, 1, bf16)
    x_grad, stacked = conv_backward(
        order, x_part, u_part, select_grad, conv_taps, conv_bias, sel_proj, log_rates, sums, needs=[z_normed],
    )

    mine, other = pick(stacked, half), pick(stacked, 1 - half)
    other = swap(other.astype(bf16), "half")
    normed_terms = (lax.dot_general(x_grad, w_x, NT, preferred_element_type=f32) + z_normed).astype(bf16)
    normed_got = collect(gate([normed_terms], other)[0])
    x_term = lax.dot_general(tokens, gate([x_grad], normed_terms)[0], TN, preferred_element_type=f32).astype(bf16)
    x_term = lax.optimization_barrier(x_term)
    x_rows = reduce_rows_by_swaps(x_term).astype(bf16)
    others = reduce_rows(jnp.concatenate(gate([z_rows, out_rows], select_grad), axis=1), "half")
    others = others.reshape(group, -1, 4 * cols)

    stacked = sum_over(mine + other.astype(f32), "fsdp")

    normed_grad = jnp.sum(normed_got.reshape(group, 2, rows_dev, width).astype(f32), axis=0)
    far_normed = swap(normed_grad[1].astype(bf16), "half")
    branch = jnp.sum(branch_got.reshape(group, 2, rows_dev, width).astype(f32), axis=0)
    far_branch = swap(gate([branch[1].astype(bf16)], far_normed)[0], "half")
    normed_grad = in_order(half, normed_grad[0], far_normed.astype(f32))
    scaled_grad = normed_grad * norm_gain
    grad_in = cotangent.astype(f32) + inverse * (
        scaled_grad - scaled * jnp.mean(scaled_grad * scaled, axis=-1, keepdims=True)
    )

    branch = in_order(half, branch[0], far_branch.astype(f32))
    block_out = (flat + branch).astype(bf16)

    x_rows = x_rows.reshape(2 * group, -1, 2 * cols)
    x_rows = lax.all_to_all(x_rows, ("half", "quarter"), split_axis=0, concat_axis=0, tiled=True)
    others = lax.all_to_all(gate([others], x_rows, far_normed)[0], "quarter", split_axis=0, concat_axis=0, tiled=True)
    x_rows = x_rows.reshape((2, group) + x_rows.shape[1:])
    grad_w_in, grad_w_out = weight_rows(x_rows, others)

    gain_part = jnp.sum(w_x.astype(f32) * x_term + w_z.astype(f32) * z_term, axis=1)
    gain = gate([gain_part], far_normed)[0]
    for axis in ("quarter", "half", "fsdp"):
        gain = sum_over(gain, axis)

    pieces = []
    at = 0
    for count in (x_proj.shape[0], low_rank, states, taps, 1, 1, 1):
        pieces.append(stacked[at : at + count])
        at += count
    xproj, dtproj, alog, convw, convb, dtbias, dskip = pieces
    return (
        block_out,
        grad_in.astype(bf16),
        gain / norm_gain,
        grad_w_in,
        convw,
        convb[0],
        xproj,
        dtproj,
        dtbias[0],
        alog,
        dskip[0],
        grad_w_out,
    )


def solution(mesh):
    fsdp, seq = mesh.devices.shape
    fine = Mesh(mesh.devices.reshape(fsdp, 2, seq // 2), ("fsdp", "half", "quarter"))
    both = ("half", "quarter")
    return jax.shard_map(
        shards,
        mesh=fine,
        in_specs=(
            P("fsdp", both, None),
            P("fsdp", both, None),
            P("fsdp"),
            P(),
            P("fsdp", None),
            P(None, both),
            P(both),
            P(None, both),
            P(None, both),
            P(both),
            P(None, both),
            P(both),
            P("fsdp", None),
        ),
        out_specs=(
            P("fsdp", both, None),
            P("fsdp", both, None),
            P(),
            P(("fsdp",) + both, None),
            P(None, both),
            P(both),
            P(None, both),
            P(None, both),
            P(both),
            P(None, both),
            P(both),
            P(("fsdp",) + both, None),
        ),
        check_vma=False,
    )
```

time: 668 us -> 587 us (0.88)
  blocking collectives: 79.1 us -> 0 us
  Pallas kernels: 102 us -> 138 us
  local copies, waits for them, and re-layouts: 80.5 us -> 57.5 us
  other arithmetic: 63.9 us -> 49.9 us
  matrix products: 90.9 us -> 79.4 us
    psum x1 -> x0, blocking collectives: 79.1 us -> none  [shards(): grad_gain = lax.psum(gain_part, ('fsdp', 'seq')) / norm_gain]
    pallas_call x0 -> x18, Pallas kernels: none -> 30.2 us  [the longest x1 12.3 us: conv_backward(): pl.pallas_call(partial(conv_backward_kernel, min(256, chan)), grid_spec=s...]
    all_to_all x3 -> x8, starting transfers between devices: 15.4 us -> 38.8 us  [the longest x4 19.9 us: spread(): lax.all_to_all(copies, 'quarter', split_axis=0, concat_axis=0, tiled=True)]
    dynamic_update_slice x31 -> x0, local copies, waits for them, and re-layouts: 23.2 us -> none  [gather_tokens(): lax.dynamic_update_slice(buffer, piece[None], (where, 0, at * (width // p...]
    ppermute x39 -> x24, starting transfers between devices: 52.3 us -> 29.6 us  [swap(): lax.ppermute(values, axis, [(index, index ^ bit) for index in range(lax.a...]
    unnamed x121 -> x141, local copies, waits for them, and re-layouts: 15.5 us -> 34.9 us
    convert_element_type x12 -> x4, other arithmetic: 23.9 us -> 6.33 us  [the longest x1 2.91 us: shards(): x_rows = reduce_rows_by_swaps(x_term).astype(bf16)]
    dot_general x13 -> x9, matrix products: 83.3 us -> 67.7 us  [the longest x1 12.6 us: shards(): gated_grad = valid * jnp.dot(cot, w_o, preferred_element_type=f32)]
  transfers between devices with their start and end apart: 49 -> 38, of which waited for: 22 -> 19; matrix products, arithmetic and copies ran while one was open for 32% -> 23% of each run, Pallas kernels for 15% -> 23%
where the time goes in v2:
time: 587 us; the launch traced here: 578 us
  waiting for transfers between devices  167 us (28%)
  Pallas kernels  138 us (24%)
  matrix products  79.4 us (14%)
  starting transfers between devices  69.3 us (12%)
  local copies, waits for them, and re-layouts  57.5 us (10%)
  other arithmetic  49.9 us (9%)
  between operations  18.2 us (3%)
    ppermute x24, waiting for transfers between devices, swap(): lax.ppermute(values, axis, [(index, index ^ bit) for index in range(lax.a...  142 us
    pallas_call x1, Pallas kernels, scan_backward(): pl.pallas_call(partial(scan_backward_kernel, low_rank, states, lanes), gr...  66.9 us
    pallas_call x1, Pallas kernels, scan_forward(): pl.pallas_call(partial(scan_forward_kernel, low_rank, states, lanes), gri...  40.5 us
    unnamed x141, local copies, waits for them, and re-layouts  34.9 us
    ppermute x24, starting transfers between devices, swap(): lax.ppermute(values, axis, [(index, index ^ bit) for index in range(lax.a...  29.6 us
    all_to_all x4, starting transfers between devices, spread(): lax.all_to_all(copies, 'quarter', split_axis=0, concat_axis=0, tiled=True)  19.9 us
    all_to_all x2, waiting for transfers between devices, collect(): lax.all_to_all(terms, 'quarter', split_axis=0, concat_axis=0, tiled=True)  16.9 us
    dot_general x1, matrix products, shards(): gated_grad = valid * jnp.dot(cot, w_o, preferred_element_type=f32)  12.6 us
  transfers between devices with their start and end apart: 38, of which 19 were waited for; matrix products, arithmetic and copies ran while one was open for 23% of the time, Pallas kernels for 23%

profile of v2, /device:TPU:0, one launch (start us, length us, event | category | flops | bytes accessed | tf_op | source)
XLA Modules:
  0.0 578.4 jit_solution(8800521097674552216)
XLA Ops:
  15.6 5.4 all-to-all-start
  22.1 2.7 collective-permute-start
  26.0 29.0 %collective-permute-done.refs_0_ = bf16[128,2048]{1,0:T(8,128)(2,1)S(1)} collective-permute-done((bf16[128,2048]{1,0:T(8,128)(2,1)}, bf16[128,2048]{1,0:T(8,128)(2,1)S(1)}, u32[]{:S(2)}, u32[]{:S(2)}) %collective-permute-start) | collective-permute-done | bytes 524320 | tf_op jit(solution)/shard_map/ppermute | solution.py:552
  58.4 2.6 broadcast_in_dim.24
  61.1 5.6 all-to-all-start.1
  66.8 2.8 collective-permute-start.2
  69.6 21.9 %collective-permute-done.1 = f32[23,512]{1,0:T(8,128)S(1)} collective-permute-done((f32[23,512]{1,0:T(8,128)S(1)}, f32[23,512]{1,0:T(8,128)S(1)}, u32[]{:S(2)}, u32[]{:S(2)}) %collective-permute-start.1) | collective-permute-done | bytes 47136 | tf_op jit(solution)/shard_map/ppermute | solution.py:552
  92.2 3.5 collective-permute-done.2
  99.2 5.3 convolution_convert_fusion.5
  107.2 6.6 %conv_forward.1 = (bf16[1024,1024]{1,0:T(8,128)(2,1)S(1)}, f32[160,1024]{1,0:T(8,128)S(1)}) custom-call(s32[8]{0:T(128)S(1)} %fusion.26.order_ref, bf16[1024,1024]{1,0:T(8,128)(2,1)S(1)} %bitcast.80, f32[4,1024]{1,0:T(4,128)S(1)} %pad_maximum_fusion.9.w_ref, f32[1,1024]{1,0:T(1,128)S(1)} %get-tuple-element.95.b_ref, bf16[160,1024]{1,0:T(8,128)(2,1)S(1)} %fusion.20.proj_ref), custom_call_target="tpu_custom_call" | custom-call | flops 335544320 | bytes 23068672 | tf_op jit(solution)/shard_map/conv_forward/pallas_call | solution.py:378
  120.4 4.6 collective-permute-done.3
  133.1 2.4 collective-permute-done.4
  143.1 4.4 all-to-all-start.3
  150.4 40.5 %scan_forward.1 = (bf16[1024,1024]{1,0:T(8,128)(2,1)S(1)}, bf16[16384,1024]{1,0:T(8,128)(2,1)}, f32[1024,1024]{1,0:T(8,128)S(1)}, bf16[1024,1024]{1,0:T(8,128)(2,1)S(1)}, f32[16,1024]{1,0:T(8,128)}) custom-call(s32[8]{0:T(128)S(1)} %fusion.26.order_ref, f32[160,1024]{1,0:T(8,128)S(1)} %copy-done.5, bf16[1024,1024]{1,0:T(8,128)(2,1)S(1)} %copy-done.11, ...), custom_call_target="tpu_custom_call" | custom-call | flops 201326592 | bytes 146800640 | tf_op jit(solution)/shard_map/scan_forward/pallas_call | solution.py:133
  195.5 2.6 broadcast_in_dim.58
  198.2 4.5 all-to-all-start.4
  204.5 4.7 interleave.2
  209.2 11.7 %fusion.1 = (bf16[1024,1024]{1,0:T(8,128)(2,1)}, f32[1024,1024]{1,0:T(8,128)}) fusion(bf16[1024,1024]{1,0:T(8,128)(2,1)} %copy-done, f32[1024]{0:T(1024)S(1)} %convert_bitcast_fusion, bf16[1024,2048]{1,0:T(8,128)(2,1)} %bitcast.92, bf16[2048,1024]{1,0:T(8,128)(2,1)} %gate.14), kind=kOutput, calls=%fused_computation.7 | convolution fusion | flops 4303355904 | bytes 16781312 | tf_op jit(solution)/shard_map/dot_general | solution.py:686
  220.9 9.5 %convolution_convert_fusion.4.refs_2_ = bf16[1024,2048]{1,0:T(8,128)(2,1)} fusion(bf16[1024,1024]{1,0:T(8,128)(2,1)} %get-tuple-element.98, bf16[2048,1024]{1,0:T(8,128)(2,1)} %all-gather.8.cloned.1.call-done), kind=kOutput, calls=%fused_computation.18 | convolution fusion | flops 4297064448 | bytes 10485760 | tf_op jit(solution)/shard_map/dot_general | solution.py:691
  230.4 4.7 interleave.3
  235.1 12.6 %fusion.3 = (bf16[1024,1024]{1,0:T(8,128)(2,1)S(1)}, bf16[1024,1024]{1,0:T(8,128)(2,1)}) fusion(bf16[1024,1024]{1,0:T(8,128)(2,1)} %copy-done, f32[1024,1024]{1,0:T(8,128)} %get-tuple-element.99.refs_1_, f32[1024]{0:T(1024)S(1)} %convert_bitcast_fusion, bf16[1024,2048]{1,0:T(8,128)(2,1)} %bitcast.95, bf16[2048,1024]{1,0:T(8,128)(2,1)} %all-gather.8.cloned.1.call-done), kind=kOutput, calls=%fused_computation.9 | convolution fusion | flops 4310695936 | bytes 18878464 | tf_op jit(solution)/shard_map/dot_general | solution.py:695
  249.0 6.4 %convolution_convert_fusion.2.refs_1_ = bf16[2048,1024]{1,0:T(8,128)(2,1)} fusion(bf16[1024,2048]{1,0:T(8,128)(2,1)S(1)} %bitcast.94, bf16[1024,1024]{1,0:T(8,128)(2,1)S(1)} %get-tuple-element.45), kind=kOutput, calls=%fused_computation.16 | convolution fusion | flops 4297064448 | bytes 10485760 | tf_op jit(solution)/shard_map/dot_general | solution.py:701
  255.4 4.9 all-to-all-start.2
  260.4 9.9 %convolution_convert_fusion.3.refs_0_ = bf16[2048,1024]{1,0:T(8,128)(2,1)} fusion(bf16[1024,2048]{1,0:T(8,128)(2,1)} %bitcast.96, bf16[1024,1024]{1,0:T(8,128)(2,1)} %get-tuple-element.98), kind=kOutput, calls=%fused_computation.17 | convolution fusion | flops 4297064448 | bytes 10485760 | tf_op jit(solution)/shard_map/dot_general | solution.py:699
  276.5 66.9 %scan_backward.1 = (f32[1024,1024]{1,0:T(8,128)S(1)}, f32[160,1024]{1,0:T(8,128)S(1)}, f32[16,1024]{1,0:T(8,128)S(1)}, f32[1,1024]{1,0:T(1,128)S(1)}, f32[1,1024...) custom-call(s32[8]{0:T(128)S(1)} %copy-done.26, f32[160,1024]{1,0:T(8,128)S(1)} %copy-done.5, ...), custom_call_target="tpu_custom_call" | custom-call | flops 503316480 | bytes 230686720 | tf_op jit(solution)/shard_map/scan_backward/pallas_call | solution.py:313
  354.7 3.0 collective-permute-done.8
  361.1 9.5 %convolution_convert_fusion.1.refs_0_ = bf16[1024,2048]{1,0:T(8,128)(2,1)} fusion(bf16[1024,1024]{1,0:T(8,128)(2,1)} %copy-done.68, bf16[2048,1024]{1,0:T(8,128)(2,1)} %gate.14), kind=kOutput, calls=%fused_computation.15 | convolution fusion | flops 4297064448 | bytes 10485760 | tf_op jit(solution)/shard_map/dot_general | solution.py:710
  370.8 12.3 %conv_backward.1 = (bf16[1024,1024]{1,0:T(8,128)(2,1)S(1)}, f32[2,320,512]{2,1,0:T(8,128)S(1)}) custom-call(s32[8]{0:T(128)S(1)} %copy-done.27, bf16[1024,1024]{1,0:T(8,128)(2,1)S(1)} %bitcast.81, bf16[1024,1024]{1,0:T(8,128)(2,1)S(1)} %bitcast.82, f32[1024,1024]{1,0:T(8,128)S(1)} %copy-done.9, f32[160,1024]{1,0:T(8,128)S(1)} %pad_maximum_fusion.6.sgrad_ref.refs_2_, ...), custom_call_target="tpu_custom_call" | custom-call | flops 671088640 | bytes 41943040 | tf_op jit(solution)/shard_map/conv_backward/pallas_call | solution.py:476
  383.3 3.3 collective-permute-start.12
  386.6 4.8 add_convert_fusion.refs_1_
  395.8 4.9 all-to-all-start.5
  401.1 7.4 %convolution_convert_fusion = bf16[2048,1024]{1,0:T(8,128)(2,1)S(1)} fusion(bf16[1024,2048]{1,0:T(8,128)(2,1)} %bitcast.93, bf16[1024,1024]{1,0:T(8,128)(2,1)} %gate.22), kind=kOutput, calls=%fused_computation.14 | convolution fusion | flops 4297064448 | bytes 10485760 | tf_op jit(solution)/shard_map/dot_general | solution.py:720
  410.9 3.1 pad_maximum_fusion.1
  415.1 3.1 convert_add_fusion
  424.4 21.4 %collective-permute-done.21 = bf16[1,512,1024]{2,1,0:T(8,128)(2,1)S(1)} collective-permute-done((bf16[1,512,1024]{2,1,0:T(8,128)(2,1)}, bf16[1,512,1024]{2,1,0:T(8,128)(2,1)S(1)}, u32[]{:S(2)}, u32[]{:S(2)}) %collective-permute-start.21) | collective-permute-done | bytes 1048608 | tf_op jit(solution)/shard_map/ppermute | solution.py:552
  445.8 2.9 add_convert_fusion.1
  448.7 16.9 %all-to-all-done.5 = bf16[4,256,2048]{2,1,0:T(8,128)(2,1)} async-done(((bf16[4,256,2048]{2,1,0:T(8,128)(2,1)}), bf16[4,256,2048]{2,1,0:T(8,128)(2,1)}, u32[]{:S(2)}, u32[]{:S(2)}) %all-to-all-start.5) | async-done | bytes 4194336 | tf_op jit(solution)/shard_map/all_to_all | solution.py:574
  465.6 5.6 all-to-all-start.6
  471.2 3.4 convert_reduce_fusion
  474.7 3.0 collective-permute-start.13
  477.7 6.4 %add_reduce_fusion.refs_0_ = f32[2048]{0:T(1024)} fusion(bf16[2048,1024]{1,0:T(8,128)(2,1)S(1)} %copy-done.32, bf16[2048,1024]{1,0:T(8,128)(2,1)} %gate.14, bf16[2048,1024]{1,0:T(8,128)(2,1)} %copy-done.37, bf16[2048,1024]{1,0:T(8,128)(2,1)} %all-gather.4.cloned.1.call-done), kind=kLoop, calls=%fused_computation | loop fusion | flops 16775168 | bytes 16785408 | tf_op jit(solution)/shard_map/reduce_sum | solution.py:747
  484.1 29.5 %collective-permute-done.13.refs_1_.refs_2_ = bf16[128,2048]{1,0:T(8,128)(2,1)S(1)} collective-permute-done((bf16[128,2048]{1,0:T(8,128)(2,1)S(1)}, bf16[128,2048]{1,0:T(8,128)(2,1)S(1)}, u32[]{:S(2)}, u32[]{:S(2)}) %collective-permute-start.13) | collective-permute-done | bytes 524320 | tf_op jit(solution)/shard_map/ppermute | solution.py:552
  515.9 3.3 convert_reduce_fusion.1
  528.9 2.6 fusion.18
  531.5 18.6 %collective-permute-done.17 = f32[2048]{0:T(1024)S(1)} collective-permute-done((f32[2048]{0:T(1024)S(1)}, f32[2048]{0:T(1024)S(1)}, u32[]{:S(2)}, u32[]{:S(2)}) %collective-permute-start.17) | collective-permute-done | bytes 8224 | tf_op jit(solution)/shard_map/ppermute | solution.py:552
  551.2 3.5 all-to-all-start.7
  562.6 3.5 fusion.13
  566.1 3.1 all-to-all-done.7.others_ref
  (276 shorter events, 109.5 us)
Async XLA Ops:
  7.2 88.6 %all-gather.4.cloned.1.call-start = ((), (), s32[]{:S(2)}) async-start(), calls=%async_computation.11 | async-start | bytes 5242880 | tf_op jit(solution)/shard_map/all_gather | solution.py:652
  15.6 41.5 %all-to-all-start = ((bf16[4,128,2048]{2,1,0:T(8,128)(2,1)}), bf16[4,128,2048]{2,1,0:T(8,128)(2,1)S(1)}, u32[]{:S(2)}, u32[]{:S(2)}) async-start(bf16[4,128,2048]{2,1,0:T(8,128)(2,1)} %broadcast_in_dim.23), calls=%async_computation | async-start | bytes 4194304 | tf_op jit(solution)/shard_map/all_to_all | solution.py:569
  21.0 188.2 %all-gather.6.cloned.1.call-start = ((), (), s32[]{:S(2)}) async-start(), calls=%async_computation.12 | async-start | bytes 5242880 | tf_op jit(solution)/shard_map/all_gather | solution.py:653
  22.1 32.9 %collective-permute-start = (bf16[128,2048]{1,0:T(8,128)(2,1)}, bf16[128,2048]{1,0:T(8,128)(2,1)S(1)}, u32[]{:S(2)}, u32[]{:S(2)}) collective-permute-start(bf16[128,2048]{1,0:T(8,128)(2,1)} %get-tuple-element.75), channel_id=1, source_target_pairs={{0,4},{4,0},{1,5},{5,1},{2,6},{6,2},{3,7},{7,3},{8,12},{12,8},{9,1... | collective-permute-start | bytes 1572872 | tf_op jit(solution)/shard_map/ppermute | solution.py:552
  61.1 36.8 %all-to-all-start.1 = ((bf16[4,128,2048]{2,1,0:T(8,128)(2,1)}), bf16[4,128,2048]{2,1,0:T(8,128)(2,1)S(1)}, u32[]{:S(2)}, u32[]{:S(2)}) async-start(bf16[4,128,2048]{2,1,0:T(8,128)(2,1)} %broadcast_in_dim.24), calls=%async_computation.1 | async-start | bytes 4194304 | tf_op jit(solution)/shard_map/all_to_all | solution.py:569
  66.7 154.2 %all-gather.8.cloned.1.call-start = ((), (), s32[]{:S(2)}) async-start(), calls=%async_computation.13 | async-start | bytes 5242880 | tf_op jit(solution)/shard_map/all_gather | solution.py:654
  66.7 24.9 %collective-permute-start.1 = (f32[23,512]{1,0:T(8,128)S(1)}, f32[23,512]{1,0:T(8,128)S(1)}, u32[]{:S(2)}, u32[]{:S(2)}) collective-permute-start(f32[23,512]{1,0:T(8,128)S(1)} %concatenate.31), channel_id=1, source_target_pairs={{0,4},{4,0},{1,5},{5,1},{2,6},{6,2},{3,7},{7,3},{8,12},{12,8},{9,1... | collective-permute-start | bytes 141320 | tf_op jit(solution)/shard_map/ppermute | solution.py:552
  66.8 82.0 %copy-start.25 = (s32[8]{0:T(128)}, s32[8]{0:T(128)S(1)}, u32[]{:S(2)}) copy-start(s32[8]{0:T(128)S(1)} %fusion.26.order_ref) | copy-start | bytes 100
  66.8 28.9 %collective-permute-start.2 = (bf16[288,512]{1,0:T(8,128)(2,1)S(1)}, bf16[288,512]{1,0:T(8,128)(2,1)S(1)}, u32[]{:S(2)}, u32[]{:S(2)}) collective-permute-start(bf16[288,512]{1,0:T(8,128)(2,1)S(1)} %pad_maximum_fusion.7), channel_id=1, source_target_pairs={{0,4},{4,0},{1,5},{5,1},{2,6},{6,2},{3,7},{7,3},{8,12},{12,8},{9,1... | collective-permute-start | bytes 884744 | tf_op jit(solution)/shard_map/ppermute | solution.py:552
  91.6 15.5 %copy-start.21 = (f32[1,1024]{1,0:T(1,128)}, f32[1,1024]{1,0:T(1,128)S(1)}, u32[]{:S(2)}) copy-start(f32[1,1024]{1,0:T(1,128)S(1)} %get-tuple-element.95.b_ref) | copy-start | bytes 12292
  91.6 57.2 %copy-start.23 = (f32[1,1024]{1,0:T(1,128)}, f32[1,1024]{1,0:T(1,128)S(1)}, u32[]{:S(2)}) copy-start(f32[1,1024]{1,0:T(1,128)S(1)} %get-tuple-element.93.skip_ref) | copy-start | bytes 12292
  115.8 9.2 %collective-permute-start.3 = (f32[160,512]{1,0:T(8,128)}, f32[160,512]{1,0:T(8,128)}, u32[]{:S(2)}, u32[]{:S(2)}) collective-permute-start(f32[160,512]{1,0:T(8,128)} %get-tuple-element.89), channel_id=1, source_target_pairs={{0,1},{1,0},{2,3},{3,2},{4,5},{5,4},{6,7},{7,6},{8,9},{9,8},{10,11... | collective-permute-start | bytes 983048 | tf_op jit(solution)/shard_map/ppermute | solution.py:552
  117.3 8.4 %collective-permute-start.5 = (f32[160,512]{1,0:T(8,128)S(1)}, f32[160,512]{1,0:T(8,128)}, u32[]{:S(2)}, u32[]{:S(2)}) collective-permute-start(f32[160,512]{1,0:T(8,128)S(1)} %get-tuple-element.90), channel_id=1, source_target_pairs={{0,2},{1,3},{2,0},{3,1},{4,6},{5,7},{6,4},{7,5},{8,10},{9,11},{10,... | collective-permute-start | bytes 983048 | tf_op jit(solution)/shard_map/ppermute | solution.py:552
  127.8 7.7 %collective-permute-start.4 = (f32[160,512]{1,0:T(8,128)}, f32[160,512]{1,0:T(8,128)}, u32[]{:S(2)}, u32[]{:S(2)}) collective-permute-start(f32[160,512]{1,0:T(8,128)} %get-tuple-element.87), channel_id=1, source_target_pairs={{0,2},{1,3},{2,0},{3,1},{4,6},{5,7},{6,4},{7,5},{8,10},{9,11},{10,... | collective-permute-start | bytes 983048 | tf_op jit(solution)/shard_map/ppermute | solution.py:552
  128.0 8.6 %collective-permute-start.6 = (f32[160,512]{1,0:T(8,128)}, f32[160,512]{1,0:T(8,128)}, u32[]{:S(2)}, u32[]{:S(2)}) collective-permute-start(f32[160,512]{1,0:T(8,128)} %get-tuple-element.88), channel_id=1, source_target_pairs={{0,1},{1,0},{2,3},{3,2},{4,5},{5,4},{6,7},{7,6},{8,9},{9,8},{10,11... | collective-permute-start | bytes 983048 | tf_op jit(solution)/shard_map/ppermute | solution.py:552
  143.1 52.4 %all-to-all-start.3 = ((bf16[4,128,2048]{2,1,0:T(8,128)(2,1)}), bf16[4,128,2048]{2,1,0:T(8,128)(2,1)}, u32[]{:S(2)}, u32[]{:S(2)}) async-start(bf16[4,128,2048]{2,1,0:T(8,128)(2,1)} %broadcast_in_dim.57), calls=%async_computation.3 | async-start | bytes 4194304 | tf_op jit(solution)/shard_map/all_to_all | solution.py:569
  147.6 47.9 %collective-permute-start.7 = (bf16[128,2048]{1,0:T(8,128)(2,1)}, bf16[128,2048]{1,0:T(8,128)(2,1)}, u32[]{:S(2)}, u32[]{:S(2)}) collective-permute-start(bf16[128,2048]{1,0:T(8,128)(2,1)} %gate.16), channel_id=1, source_target_pairs={{0,4},{4,0},{1,5},{5,1},{2,6},{6,2},{3,7},{7,3},{8,12},{12,8},{9,1... | collective-permute-start | bytes 1572872 | tf_op jit(solution)/shard_map/ppermute | solution.py:552
  198.2 32.2 %all-to-all-start.4 = ((bf16[4,128,2048]{2,1,0:T(8,128)(2,1)}), bf16[4,128,2048]{2,1,0:T(8,128)(2,1)}, u32[]{:S(2)}, u32[]{:S(2)}) async-start(bf16[4,128,2048]{2,1,0:T(8,128)(2,1)} %broadcast_in_dim.58), calls=%async_computation.4 | async-start | bytes 4194304 | tf_op jit(solution)/shard_map/all_to_all | solution.py:569
  202.7 208.2 %reduce-scatter.4.cloned.1.call-start = ((), (), s32[]{:S(2)}) async-start(), calls=%async_computation.14 | async-start | bytes 5242880 | tf_op jit(solution)/shard_map/reduce_scatter | solution.py:609
  235.1 13.9 %copy-start.45 = (bf16[4,2,128,2048]{3,2,1,0:T(8,128)(2,1)S(1)}, bf16[4,2,128,2048]{3,2,1,0:T(8,128)(2,1)}, u32[]{:S(2)}) copy-start(bf16[4,2,128,2048]{3,2,1,0:T(8,128)(2,1)} %interleave.2) | copy-start | bytes 12582916
  255.4 92.7 %all-to-all-start.2 = ((bf16[4,256,2048]{2,1,0:T(8,128)(2,1)}), bf16[4,256,2048]{2,1,0:T(8,128)(2,1)}, u32[]{:S(2)}, u32[]{:S(2)}) async-start(bf16[4,256,2048]{2,1,0:T(8,128)(2,1)} %bitcast.84), calls=%async_computation.2 | async-start | bytes 8388608 | tf_op jit(solution)/shard_map/all_to_all | solution.py:574
  260.3 150.6 %reduce-scatter.6.cloned.1.call-start = ((), (), s32[]{:S(2)}) async-start(), calls=%async_computation.15 | async-start | bytes 5242880 | tf_op jit(solution)/shard_map/reduce_scatter | solution.py:609
  349.3 5.4 collective-permute-start.10
  351.4 6.3 %collective-permute-start.8 = (bf16[160,512]{1,0:T(8,128)(2,1)S(1)}, bf16[160,512]{1,0:T(8,128)(2,1)S(1)}, u32[]{:S(2)}, u32[]{:S(2)}) collective-permute-start(bf16[160,512]{1,0:T(8,128)(2,1)S(1)} %get-tuple-element.83), channel_id=1, source_target_pairs={{0,1},{1,0},{2,3},{3,2},{4,5},{5,4},{6,7},{7,6},{8,9},{9,8},{10,11... | collective-permute-start | bytes 491528 | tf_op jit(solution)/shard_map/ppermute | solution.py:552
  358.8 11.7 %collective-permute-start.11 = (bf16[160,512]{1,0:T(8,128)(2,1)S(1)}, bf16[160,512]{1,0:T(8,128)(2,1)S(1)}, u32[]{:S(2)}, u32[]{:S(2)}) collective-permute-start(bf16[160,512]{1,0:T(8,128)(2,1)S(1)} %get-tuple-element.82), channel_id=1, source_target_pairs={{0,1},{1,0},{2,3},{3,2},{4,5},{5,4},{6,7},{7,6},{8,9},{9,8},{10,11... | collective-permute-start | bytes 491528 | tf_op jit(solution)/shard_map/ppermute | solution.py:552
  360.4 10.2 %collective-permute-start.9 = (bf16[160,512]{1,0:T(8,128)(2,1)S(1)}, bf16[160,512]{1,0:T(8,128)(2,1)S(1)}, u32[]{:S(2)}, u32[]{:S(2)}) collective-permute-start(bf16[160,512]{1,0:T(8,128)(2,1)S(1)} %get-tuple-element.81), channel_id=1, source_target_pairs={{0,2},{1,3},{2,0},{3,1},{4,6},{5,7},{6,4},{7,5},{8,10},{9,11},{10,... | collective-permute-start | bytes 491528 | tf_op jit(solution)/shard_map/ppermute | solution.py:552
  370.8 15.7 %copy-start.47 = (bf16[2048,1024]{1,0:T(8,128)(2,1)S(1)}, bf16[2048,1024]{1,0:T(8,128)(2,1)}, u32[]{:S(2)}) copy-start(bf16[2048,1024]{1,0:T(8,128)(2,1)} %all-gather.4.cloned.1.call-done) | copy-start | bytes 12582916
  370.8 15.7 %copy-start.48 = (bf16[1024,2048]{1,0:T(8,128)(2,1)S(1)}, bf16[1024,2048]{1,0:T(8,128)(2,1)}, u32[]{:S(2)}) copy-start(bf16[1024,2048]{1,0:T(8,128)(2,1)} %convolution_convert_fusion.1.refs_0_) | copy-start | bytes 12582916
  383.3 11.8 %collective-permute-start.12 = (bf16[320,512]{1,0:T(8,128)(2,1)S(1)}, bf16[320,512]{1,0:T(8,128)(2,1)S(1)}, u32[]{:S(2)}, u32[]{:S(2)}) collective-permute-start(bf16[320,512]{1,0:T(8,128)(2,1)S(1)} %fusion.21), channel_id=1, source_target_pairs={{0,4},{4,0},{1,5},{5,1},{2,6},{6,2},{3,7},{7,3},{8,12},{12,8},{9,1... | collective-permute-start | bytes 983048 | tf_op jit(solution)/shard_map/ppermute | solution.py:552
  395.8 69.7 %all-to-all-start.5 = ((bf16[4,256,2048]{2,1,0:T(8,128)(2,1)}), bf16[4,256,2048]{2,1,0:T(8,128)(2,1)}, u32[]{:S(2)}, u32[]{:S(2)}) async-start(bf16[4,256,2048]{2,1,0:T(8,128)(2,1)} %bitcast.85), calls=%async_computation.5 | async-start | bytes 8388608 | tf_op jit(solution)/shard_map/all_to_all | solution.py:574
  400.7 149.4 %reduce-scatter.8.cloned.1.call-start = ((), (), s32[]{:S(2)}) async-start(), calls=%async_computation.16 | async-start | bytes 3145728 | tf_op jit(solution)/shard_map/reduce_scatter | solution.py:609
  410.8 4.4 collective-permute-start.20
  419.5 26.2 %collective-permute-start.21 = (bf16[1,512,1024]{2,1,0:T(8,128)(2,1)}, bf16[1,512,1024]{2,1,0:T(8,128)(2,1)S(1)}, u32[]{:S(2)}, u32[]{:S(2)}) collective-permute-start(bf16[1,512,1024]{2,1,0:T(8,128)(2,1)} %dynamic-slice_convert_fusion), channel_id=1, source_target_pairs={{0,16},{8,24},{16,0},{24,8},{1,17},{9,25},{17,1},{25,9},{2,18},{10... | collective-permute-start | bytes 3145736 | tf_op jit(solution)/shard_map/ppermute | solution.py:552
  421.1 2.2 collective-permute-start.22
  423.4 97.9 %collective-permute-start.23 = (f32[320,512]{1,0:T(8,128)S(1)}, f32[320,512]{1,0:T(8,128)}, u32[]{:S(2)}, u32[]{:S(2)}) collective-permute-start(f32[320,512]{1,0:T(8,128)S(1)} %add.242), channel_id=1, source_target_pairs={{0,16},{8,24},{16,0},{24,8},{1,17},{9,25},{17,1},{25,9},{2,18},{10... | collective-permute-start | bytes 1966088 | tf_op jit(solution)/shard_map/ppermute | solution.py:552
  465.6 84.6 %all-to-all-start.6 = ((bf16[8,64,1024]{2,1,0:T(8,128)(2,1)}), bf16[8,64,1024]{2,1,0:T(8,128)(2,1)S(1)}, u32[]{:S(2)}, u32[]{:S(2)}) async-start(bf16[8,64,1024]{2,1,0:T(8,128)(2,1)} %bitcast.30), calls=%async_computation.6 | async-start | bytes 2097152 | tf_op jit(solution)/shard_map/all_to_all | solution.py:742
  474.7 38.9 %collective-permute-start.13 = (bf16[128,2048]{1,0:T(8,128)(2,1)S(1)}, bf16[128,2048]{1,0:T(8,128)(2,1)S(1)}, u32[]{:S(2)}, u32[]{:S(2)}) collective-permute-start(bf16[128,2048]{1,0:T(8,128)(2,1)S(1)} %slice.121), channel_id=1, source_target_pairs={{0,4},{4,0},{1,5},{5,1},{2,6},{6,2},{3,7},{7,3},{8,12},{12,8},{9,1... | collective-permute-start | bytes 1572872 | tf_op jit(solution)/shard_map/ppermute | solution.py:552
  514.4 8.1 %collective-permute-start.15 = (f32[2048]{0:T(1024)}, f32[2048]{0:T(1024)S(1)}, u32[]{:S(2)}, u32[]{:S(2)}) collective-permute-start(f32[2048]{0:T(1024)} %gate.23), channel_id=1, source_target_pairs={{0,1},{1,0},{2,3},{3,2},{4,5},{5,4},{6,7},{7,6},{8,9},{9,8},{10,11... | collective-permute-start | bytes 24584 | tf_op jit(solution)/shard_map/ppermute | solution.py:552
  522.6 5.3 collective-permute-start.16
  525.9 35.0 %collective-permute-start.14 = (bf16[128,2048]{1,0:T(8,128)(2,1)}, bf16[128,2048]{1,0:T(8,128)(2,1)}, u32[]{:S(2)}, u32[]{:S(2)}) collective-permute-start(bf16[128,2048]{1,0:T(8,128)(2,1)} %gate.21), channel_id=1, source_target_pairs={{0,4},{4,0},{1,5},{5,1},{2,6},{6,2},{3,7},{7,3},{8,12},{12,8},{9,1... | collective-permute-start | bytes 1572872 | tf_op jit(solution)/shard_map/ppermute | solution.py:552
  527.9 26.8 %copy-start.38 = (bf16[2,128,2048]{2,1,0:T(8,128)(2,1)S(1)}, bf16[2,128,2048]{2,1,0:T(8,128)(2,1)}, u32[]{:S(2)}) copy-start(bf16[2,128,2048]{2,1,0:T(8,128)(2,1)} %param.13) | copy-start | bytes 3145732
  527.9 26.8 %copy-start.58 = (f32[2048]{0:T(1024)S(1)}, f32[2048]{0:T(1024)}, u32[]{:S(2)}) copy-start(f32[2048]{0:T(1024)} %param.16) | copy-start | bytes 24580
  527.9 26.8 %copy-start.62 = (f32[2,128]{1,0:T(2,128)S(1)}, f32[2,128]{1,0:T(2,128)}, u32[]{:S(2)}) copy-start(f32[2,128]{1,0:T(2,128)} %copy-done.61) | copy-start | bytes 3076
  527.9 22.2 %collective-permute-start.17 = (f32[2048]{0:T(1024)S(1)}, f32[2048]{0:T(1024)S(1)}, u32[]{:S(2)}, u32[]{:S(2)}) collective-permute-start(f32[2048]{0:T(1024)S(1)} %add.231), channel_id=1, source_target_pairs={{0,4},{4,0},{1,5},{5,1},{2,6},{6,2},{3,7},{7,3},{8,12},{12,8},{9,1... | collective-permute-start | bytes 24584 | tf_op jit(solution)/shard_map/ppermute | solution.py:552
  531.5 31.0 %copy-start.40 = (f32[1,128,2048]{2,1,0:T(8,128)}, f32[1,128,2048]{2,1,0:T(8,128)S(1)}, u32[]{:S(2)}) copy-start(f32[1,128,2048]{2,1,0:T(8,128)S(1)} %get-tuple-element.66) | copy-start | bytes 3145732
  550.1 6.5 %collective-permute-start.18 = (f32[2048]{0:T(1024)S(1)}, f32[2048]{0:T(1024)S(1)}, u32[]{:S(2)}, u32[]{:S(2)}) collective-permute-start(f32[2048]{0:T(1024)S(1)} %add.232), channel_id=1, source_target_pairs={{0,8},{8,0},{16,24},{24,16},{1,9},{9,1},{17,25},{25,17},{2,10},{10... | collective-permute-start | bytes 24584 | tf_op jit(solution)/shard_map/ppermute | solution.py:552
  551.2 18.1 %all-to-all-start.7 = ((bf16[4,64,2048]{2,1,0:T(8,128)(2,1)}), bf16[4,64,2048]{2,1,0:T(8,128)(2,1)S(1)}, u32[]{:S(2)}, u32[]{:S(2)}) async-start(bf16[4,64,2048]{2,1,0:T(8,128)(2,1)} %gate.25), calls=%async_computation.10 | async-start | bytes 2097152 | tf_op jit(solution)/shard_map/all_to_all | solution.py:743
  556.6 3.7 collective-permute-start.19
  (59 other events, 307.5 us)
Sparse Core Ops, SparseCore 0:
  13.3 37.1 all-gather.3
  52.6 34.4 all-gather.5
  120.5 33.6 all-gather.7
  255.6 46.3 reduce-scatter.3
  304.5 44.5 reduce-scatter.5
  414.1 84.2 reduce-scatter.7
